TPU v7x, 512 devices: a whole 4x4x16 slice. The times are simulated.
512 devices in a mesh: rows: 64 (over z, x), cols: 8 (over y, core).
Axes of the slice: x: 4, y: 4, z: 16, core: 2. Of those that a mesh axis runs over, the one named last changes fastest.
Arguments:
- panel: float32 [2048, 32768], P('rows', 'cols'), may hold values from -0.03125 to 0.03125
- solved: float32 [32768, 64], P('cols'), may hold values from -6 to 6
- sketch: float32 [2048, 64], P('rows'), may hold values from -6 to 6
- inverses: float32 [2, 1024, 1024], P(None, 'rows', 'cols'), may hold values from -2 to 2, as said below
- coupling: float32 [1024, 1024], P('rows', 'cols'), may hold values from -0.1875 to 0.1875
- design: bfloat16 [131072, 2048], P('rows', 'cols'), may hold values from -0.125 to 0.125
- prior: float32 [131072, 64], P(('rows', 'cols')), may hold values from -6 to 6
Outputs:
- block_solution: float32 [2048, 64], P('rows')
- leverage: float32 [131072], P(('rows', 'cols'))
Inputs may be any that keep to these rules, and one draw needn't show every extreme that they name: `inverses`: each of the two blocks is upper triangular with a positive diagonal.
All inputs are finite; a program needn't handle non-finite values.
Results may differ from a plain program's by a relative error of at most 0.00063.
Values sent between devices are 32-bit elements; how exact they have to be, the bound alone decides.
No kernel may reach another device: no remote copies, remote signals or barrier semaphores. Data moves between devices by JAX's collectives and lax.ppermute only.
A program may use at most 64 MiB of HBM per device.

v0:
```python
import jax
import jax.numpy as jnp
from jax import lax
from jax.sharding import PartitionSpec as P


def sent_to_all(value, axis):
    count = lax.axis_size(axis)
    return lax.all_to_all(
        jnp.broadcast_to(value[None], (count, *value.shape)), axis, 0, 0, tiled=True
    )


def of_everyone(value, axis):
    everything = sent_to_all(value, axis)
    return jnp.sum(everything, axis=0)


def joined_along(tiles, dim):
    tiles = jnp.moveaxis(tiles, 0, dim)
    shape = tiles.shape
    return tiles.reshape(*shape[:dim], shape[dim] * shape[dim + 1], *shape[dim + 2 :])


def gather_directly(value, axis, dim):
    tiles = sent_to_all(value, axis)
    return joined_along(tiles, dim)


def split_up(value, dim, count):
    before, after = (value.shape[:dim], value.shape[dim + 1 :])
    return jnp.moveaxis(value.reshape(*before, count, -1, *after), dim, 0)


def sum_at_owner(value, axis, dim):
    tiles = split_up(value, dim, lax.axis_size(axis))
    arrived = lax.all_to_all(tiles, axis, split_axis=0, concat_axis=0, tiled=True)
    return arrived.sum(axis=0)


def assemble(term):
    rows_here = of_everyone(term, "cols")
    return gather_directly(rows_here, "rows", 0)


def local(panel, solved, sketch, inverses, coupling, design, prior):
    highest = lax.Precision.HIGHEST
    partial_value = jnp.dot(panel, solved, precision=highest)
    local_right = sketch - of_everyone(partial_value, "cols")
    right = gather_directly(local_right, "rows", 0)
    blocks = right.shape[0] // 2
    width = inverses.shape[2]
    column = lax.axis_index("cols")
    offset = column * width

    def piece(vector):
        return lax.dynamic_slice_in_dim(vector, offset, width, 0)

    right_first = right[:blocks]
    right_last = right[blocks:]
    y_last = assemble(jnp.dot(inverses[1], piece(right_last), precision=highest))
    bent = assemble(jnp.dot(coupling, piece(y_last), precision=highest))
    y_first = assemble(jnp.dot(inverses[0], piece(right_first - bent), precision=highest))
    solution = jnp.concatenate([y_first, y_last], axis=0)
    own_rows = sketch.shape[0]
    block_solution = lax.dynamic_slice_in_dim(
        solution, lax.axis_index("rows") * own_rows, own_rows, 0
    )
    design_cols = design.shape[1]
    rounded = lax.dynamic_slice_in_dim(solution, column * design_cols, design_cols, 0).astype(
        jnp.bfloat16
    )
    mine = sum_at_owner(jnp.dot(design, rounded, preferred_element_type=jnp.float32), "cols", 0)
    product = prior + mine
    leverage = jnp.mean(product * product, axis=1)
    return (block_solution, leverage)


def solution(mesh):
    in_specs = (
        P("rows", "cols"),
        P("cols", None),
        P("rows", None),
        P(None, "rows", "cols"),
        P("rows", "cols"),
        P("rows", "cols"),
        P(("rows", "cols"), None),
    )
    out_specs = (P("rows", None), P(("rows", "cols")))
    return jax.shard_map(local, mesh=mesh, in_specs=in_specs, out_specs=out_specs, check_vma=False)
```

profile of v0, /device:TPU:1, one launch (start us, length us, event | category | flops | bytes accessed | tf_op | source)
XLA Modules:
  0.0 203.5 jit_solution(11372582188372060380)
XLA Ops:
  0.6 0.0 copy-start
  0.6 2.4 %fusion.18 = f32[32,64]{1,0:T(8,128)S(1)} fusion(f32[32,4096]{1,0:T(8,128)} %param.7, f32[4096,64]{0,1:T(8,128)} %param.8), kind=kOutput, calls=%fused_computation.28 | convolution fusion | flops 100663296 | bytes 1581056 | tf_op jit(solution)/shard_map/dot_general | solution.py:48
  3.1 0.1 reshape.31
  3.2 14.1 %all_to_all.45 = f32[8,1,2048]{2,1,0:T(1,128)S(1)} all-to-all(f32[8,1,2048]{2,1,0:T(1,128)S(1)} %reshape.31), channel_id=1, replica_groups=mesh['rows'=64,'cols'=8] {'cols'}, dimensions={0} | all-to-all | bytes 131072 | tf_op jit(solution)/shard_map/all_to_all | solution.py:9
  17.3 0.5 broadcast.9
  17.8 0.8 reduce
  18.6 0.1 reshape.32
  18.7 0.0 copy-start.2
  18.7 0.7 copy-done.2
  19.4 0.1 broadcast_in_dim.17
  19.6 1.4 reshape.33
  21.0 14.8 %all-to-all-start.1 = ((f32[64,1,2048]{2,1,0:T(1,128)}), f32[64,1,2048]{2,1,0:T(1,128)S(1)}, u32[]{:S(2)}, u32[]{:S(2)}) async-start(f32[64,1,2048]{2,1,0:T(1,128)} %reshape.33), calls=%async_computation.1 | async-start | bytes 1048576 | tf_op jit(solution)/shard_map/all_to_all | solution.py:9
  35.8 29.5 %all-to-all-done.1 = f32[64,1,2048]{2,1,0:T(1,128)S(1)} async-done(((f32[64,1,2048]{2,1,0:T(1,128)}), f32[64,1,2048]{2,1,0:T(1,128)S(1)}, u32[]{:S(2)}, u32[]{:S(2)}) %all-to-all-start.1) | async-done | bytes 524320 | tf_op jit(solution)/shard_map/all_to_all | solution.py:9
  65.3 1.9 reduce.1
  67.2 0.4 reshape.34
  67.6 0.0 copy-start.3
  67.6 0.1 fusion.17
  67.7 0.6 copy-done.3
  68.4 0.2 convolution_bitcast_fusion.2
  68.5 0.1 reshape.35
  68.6 11.4 %all_to_all.46 = f32[8,1,1024]{2,1,0:T(1,128)S(1)} all-to-all(f32[8,1,1024]{2,1,0:T(1,128)S(1)} %reshape.35), channel_id=1, replica_groups=mesh['rows'=64,'cols'=8] {'cols'}, dimensions={0} | all-to-all | bytes 65536 | tf_op jit(solution)/shard_map/all_to_all | solution.py:9
  80.0 0.7 reduce.2
  80.7 0.1 reshape.36
  80.9 0.3 reshape.37
  81.2 24.6 %all_to_all.47 = f32[64,1,1024]{2,1,0:T(1,128)S(1)} all-to-all(f32[64,1,1024]{2,1,0:T(1,128)S(1)} %reshape.37), channel_id=1, replica_groups=mesh['rows'=64,'cols'=8] {'rows'}, dimensions={0} | all-to-all | bytes 524288 | tf_op jit(solution)/shard_map/all_to_all | solution.py:9
  105.8 1.3 reduce.3
  107.0 0.0 copy-start.4
  107.0 0.1 reshape.38
  107.2 0.6 copy-done.4
  107.7 0.2 convolution_bitcast_fusion.1
  107.9 0.1 reshape.39
  108.0 11.3 %all_to_all.48 = f32[8,1,1024]{2,1,0:T(1,128)S(1)} all-to-all(f32[8,1,1024]{2,1,0:T(1,128)S(1)} %reshape.39), channel_id=1, replica_groups=mesh['rows'=64,'cols'=8] {'cols'}, dimensions={0} | all-to-all | bytes 65536 | tf_op jit(solution)/shard_map/all_to_all | solution.py:9
  119.3 0.7 reduce.4
  120.0 0.1 reshape.40
  120.2 0.3 reshape.41
  120.5 23.7 %all_to_all.49 = f32[64,1,1024]{2,1,0:T(1,128)S(1)} all-to-all(f32[64,1,1024]{2,1,0:T(1,128)S(1)} %reshape.41), channel_id=1, replica_groups=mesh['rows'=64,'cols'=8] {'rows'}, dimensions={0} | all-to-all | bytes 524288 | tf_op jit(solution)/shard_map/all_to_all | solution.py:9
  144.2 1.3 reduce.5
  145.5 0.1 reshape.42
  145.6 0.2 convolution_bitcast_fusion
  145.8 0.1 reshape.43
  145.9 11.3 %all_to_all.50 = f32[8,1,1024]{2,1,0:T(1,128)S(1)} all-to-all(f32[8,1,1024]{2,1,0:T(1,128)S(1)} %reshape.43), channel_id=1, replica_groups=mesh['rows'=64,'cols'=8] {'cols'}, dimensions={0} | all-to-all | bytes 65536 | tf_op jit(solution)/shard_map/all_to_all | solution.py:9
  157.2 0.7 reduce.6
  157.9 0.1 reshape.44
  158.0 1.0 reshape.45
  159.1 4.7 %all-to-all-start.7 = ((f32[64,1,1024]{2,1,0:T(1,128)}), f32[64,1,1024]{2,1,0:T(1,128)S(1)}, u32[]{:S(2)}, u32[]{:S(2)}) async-start(f32[64,1,1024]{2,1,0:T(1,128)} %reshape.45), calls=%async_computation.7 | async-start | bytes 524288 | tf_op jit(solution)/shard_map/all_to_all | solution.py:9
  163.7 19.2 %all-to-all-done.7 = f32[64,1,1024]{2,1,0:T(1,128)S(1)} async-done(((f32[64,1,1024]{2,1,0:T(1,128)}), f32[64,1,1024]{2,1,0:T(1,128)S(1)}, u32[]{:S(2)}, u32[]{:S(2)}) %all-to-all-start.7) | async-done | bytes 262176 | tf_op jit(solution)/shard_map/all_to_all | solution.py:9
  182.9 1.3 reduce.7
  184.2 0.1 reshape.46
  184.4 0.0 copy-done
  184.4 0.5 fusion.2
  184.9 0.8 copy.13
  185.7 7.6 %all-to-all-start.8 = ((f32[8,256,64]{1,2,0:T(8,128)}), f32[8,256,64]{1,2,0:T(8,128)S(1)}, u32[]{:S(2)}, u32[]{:S(2)}) async-start(f32[8,256,64]{1,2,0:T(8,128)} %bitcast.25), calls=%async_computation.8 | async-start | bytes 1048576 | tf_op jit(solution)/shard_map/all_to_all | solution.py:37
  193.3 0.6 fusion.7
  193.9 0.0 copy-start.1
  193.9 8.9 %all-to-all-done.8 = f32[8,256,64]{1,2,0:T(8,128)S(1)} async-done(((f32[8,256,64]{1,2,0:T(8,128)}), f32[8,256,64]{1,2,0:T(8,128)S(1)}, u32[]{:S(2)}, u32[]{:S(2)}) %all-to-all-start.8) | async-done | bytes 524320 | tf_op jit(solution)/shard_map/all_to_all | solution.py:37
  202.9 0.0 copy-done.1
  202.9 0.6 broadcast_multiply_fusion
  (14 shorter events, 0.3 us)
Async XLA Ops:
  0.6 183.7 %copy-start = (bf16[2048,256]{1,0:T(8,128)(2,1)S(1)}, bf16[2048,256]{1,0:T(8,128)(2,1)}, u32[]{:S(2)}) copy-start(bf16[2048,256]{1,0:T(8,128)(2,1)} %param.12) | copy-start | bytes 3145732
  18.7 0.7 copy-start.2
  21.0 44.3 %all-to-all-start.1 = ((f32[64,1,2048]{2,1,0:T(1,128)}), f32[64,1,2048]{2,1,0:T(1,128)S(1)}, u32[]{:S(2)}, u32[]{:S(2)}) async-start(f32[64,1,2048]{2,1,0:T(1,128)} %reshape.33), calls=%async_computation.1 | async-start | bytes 1048576 | tf_op jit(solution)/shard_map/all_to_all | solution.py:9
  67.6 0.7 copy-start.3
  107.0 0.7 copy-start.4
  159.1 23.9 %all-to-all-start.7 = ((f32[64,1,1024]{2,1,0:T(1,128)}), f32[64,1,1024]{2,1,0:T(1,128)S(1)}, u32[]{:S(2)}, u32[]{:S(2)}) async-start(f32[64,1,1024]{2,1,0:T(1,128)} %reshape.45), calls=%async_computation.7 | async-start | bytes 524288 | tf_op jit(solution)/shard_map/all_to_all | solution.py:9
  185.7 17.1 %all-to-all-start.8 = ((f32[8,256,64]{1,2,0:T(8,128)}), f32[8,256,64]{1,2,0:T(8,128)S(1)}, u32[]{:S(2)}, u32[]{:S(2)}) async-start(f32[8,256,64]{1,2,0:T(8,128)} %bitcast.25), calls=%async_computation.8 | async-start | bytes 1048576 | tf_op jit(solution)/shard_map/all_to_all | solution.py:37
  193.9 8.9 %copy-start.1 = (f32[256,64]{0,1:T(8,128)S(1)}, f32[256,64]{0,1:T(8,128)}, u32[]{:S(2)}) copy-start(f32[256,64]{0,1:T(8,128)} %param.13) | copy-start | bytes 196612
where the time goes:
time: 204 us; the launch traced here: 203 us
  blocking collectives  96.3 us (47%)
  waiting for transfers between devices  57.6 us (28%)
  starting transfers between devices  27.1 us (13%)
  other arithmetic  9.93 us (5%)
  local copies, waits for them, and re-layouts  8.28 us (4%)
  matrix products  3.39 us (2%)
    all_to_all x6, blocking collectives, sent_to_all(): lax.all_to_all(jnp.broadcast_to(value[None], (count, *value.shape)), axis...  96.3 us
    all_to_all x2, waiting for transfers between devices, sent_to_all(): lax.all_to_all(jnp.broadcast_to(value[None], (count, *value.shape)), axis...  48.7 us
    all_to_all x2, starting transfers between devices, sent_to_all(): lax.all_to_all(jnp.broadcast_to(value[None], (count, *value.shape)), axis...  19.5 us
    all_to_all x1, waiting for transfers between devices, sum_at_owner(): lax.all_to_all(tiles, axis, split_axis=0, concat_axis=0, tiled=True)  8.88 us
    all_to_all x8, other arithmetic, sent_to_all(): lax.all_to_all(jnp.broadcast_to(value[None], (count, *value.shape)), axis...  8.61 us
    all_to_all x1, starting transfers between devices, sum_at_owner(): lax.all_to_all(tiles, axis, split_axis=0, concat_axis=0, tiled=True)  7.61 us
    unnamed x26, local copies, waits for them, and re-layouts  6.56 us
  transfers between devices with their start and end apart: 3, of which 3 were waited for; matrix products, arithmetic and copies ran while one was open for 0% of the time, Pallas kernels for 0%

commit v1 on v0

v1 whole, which is shorter than its diff:
```python
import jax
import jax.numpy as jnp
from jax import lax
from jax.sharding import Mesh
from jax.sharding import PartitionSpec as P

HIGHEST = lax.Precision.HIGHEST


def dot(a, b):
    return jnp.dot(a, b, precision=HIGHEST)


def exchange(value, axes):
    return lax.all_to_all(value, axes, 0, 0, tiled=True)


def to_all(value, axes, count):
    return exchange(jnp.broadcast_to(value[None], (count, *value.shape)), axes)


def packed(value):
    half = value.shape[-2] // 2
    return jnp.concatenate([value[..., :half, :], value[..., half:, :]], axis=-1)


def unpacked(value):
    return jnp.concatenate([value[..., :64], value[..., 64:]], axis=-2)


def local(panel, solved, sketch, inverses, coupling, design, prior):
    zh, zl, x, c = (lax.axis_index(name) for name in ("zh", "zl", "x", "c"))

    start = jnp.where(c == 0, sketch, 0.0) - dot(panel, solved)
    rows = start.reshape(8, 2, 128)

    def by_subset(block):
        return block.reshape(16, 4, 8, 4).transpose(2, 0, 1, 3).reshape(8, 2, 128)

    pieces = jnp.concatenate([rows, by_subset(inverses[1]), by_subset(inverses[0])], axis=1)
    turned = coupling.reshape(4, 4, 2, 4, 16).transpose(3, 0, 1, 2, 4).reshape(4, 1, 4, 1, 128)
    message = jnp.concatenate(
        [
            jnp.broadcast_to(pieces[None], (4, 8, 6, 128)),
            jnp.broadcast_to(turned, (4, 2, 4, 1, 128)).reshape(4, 8, 1, 128),
        ],
        axis=2,
    )
    got = exchange(message.reshape(32, 7, 128), ("x", "c")).reshape(4, 8, 7, 128)
    right = got[:, :, :2].sum(axis=1).reshape(16, 64)
    mine = lax.dynamic_index_in_dim(got, x, 0, keepdims=False)

    def joined(block):
        return block.reshape(8, 16, 16).transpose(1, 0, 2).reshape(16, 128)

    last_rows = joined(mine[:, 2:4])
    first_rows = joined(mine[:, 4:6])
    turned = lax.dynamic_index_in_dim(
        got[:, :, 6].reshape(2, 2, 8, 128), c // 4, 1, keepdims=False
    )
    turned = turned.reshape(2, 8, 4, 2, 2, 8).transpose(4, 0, 2, 1, 3, 5).reshape(2, 8, 128)

    common = packed(right)
    message = jnp.stack(
        [
            jnp.concatenate([common, last_rows[8 * h : 8 * h + 8], turned[h], first_rows])
            for h in range(2)
        ]
    )
    message = jnp.broadcast_to(message[None], (8, 2, 40, 128)).reshape(16, 40, 128)
    got = exchange(message, ("zh", "zl"))
    right = unpacked(got[:, :8])
    right_first = right[:8].reshape(128, 64)
    right_last = right[8:].reshape(128, 64)
    inverse_last = got[:, 8:16].reshape(128, 128)
    couple = got[:, 16:24].reshape(128, 128)
    inverse_first = got[:, 24:40].reshape(256, 128)

    parts = to_all(packed(dot(inverse_last, right_last)), "c", 8)
    y_last = unpacked(parts.sum(axis=0))

    bent = packed(dot(couple, y_last))
    piece = packed(lax.dynamic_slice_in_dim(y_last, 32 * (c % 4), 32, 0))
    parts = to_all(jnp.concatenate([bent, piece]), ("zl", "x"), 8)
    bent = unpacked(parts[:, :64].sum(axis=0))
    block_last = unpacked(parts[:, 64:]).reshape(2, 4, 4, 8, 64)
    block_last = block_last.transpose(2, 1, 0, 3, 4).reshape(256, 64)

    terms = packed(dot(inverse_first, right_first - bent).reshape(4, 64, 64))
    terms = jnp.broadcast_to(terms[None], (8, 4, 32, 128)).reshape(32, 32, 128)
    parts = exchange(terms, ("x", "c")).reshape(4, 8, 32, 128)
    block_first = unpacked(parts.sum(axis=1)).reshape(4, 4, 16, 64)
    block_first = block_first.transpose(1, 0, 2, 3).reshape(256, 64)
    block = jnp.where(c < 4, block_first, block_last)

    rounded = block.astype(jnp.bfloat16)
    product = jnp.dot(design, rounded, preferred_element_type=jnp.float32)
    product = packed(product.reshape(8, 256, 64))
    own = packed(lax.dynamic_slice_in_dim(block, 32 * (4 * zl + x), 32, 0))
    message = jnp.concatenate(
        [product, jnp.broadcast_to(own[None], (8, 16, 128))], axis=1
    )
    got = exchange(message, "c")
    block_solution = unpacked(lax.dynamic_index_in_dim(got, zh, 0, keepdims=False)[128:])
    total = packed(prior) + got[:, :128].sum(axis=0)
    leverage = (total * total).reshape(128, 2, 64).sum(axis=2).T.reshape(256) * (1.0 / 64)
    return block_solution, leverage


def solution(mesh):
    fine = Mesh(mesh.devices.reshape(8, 2, 4, 8), ("zh", "zl", "x", "c"))
    r = ("zh", "zl", "x")
    in_specs = (
        P(r, "c"),
        P("c", None),
        P(r, None),
        P(None, r, "c"),
        P(r, "c"),
        P(r, "c"),
        P((*r, "c"), None),
    )
    out_specs = (P(r, None), P((*r, "c")))
    return jax.shard_map(local, mesh=fine, in_specs=in_specs, out_specs=out_specs, check_vma=False)
```

time: 204 us -> 122 us (0.60)
  blocking collectives: 96.3 us -> 28.1 us
  waiting for transfers between devices: 57.6 us -> 42.1 us
  other arithmetic: 9.93 us -> 3.6 us
  starting transfers between devices: 27.1 us -> 33.4 us
    all_to_all x6 -> x1, blocking collectives: 96.3 us -> 28.1 us  [exchange(): return lax.all_to_all(value, axes, 0, 0, tiled=True)]
    all_to_all x3 -> x5, waiting for transfers between devices: 57.6 us -> 42.1 us  [exchange(): return lax.all_to_all(value, axes, 0, 0, tiled=True)]
    all_to_all x8 -> x0, other arithmetic: 8.61 us -> none  [sent_to_all(): lax.all_to_all(jnp.broadcast_to(value[None], (count, *value.shape)), axis...]
    all_to_all x3 -> x5, starting transfers between devices: 27.1 us -> 33.4 us  [exchange(): return lax.all_to_all(value, axes, 0, 0, tiled=True)]
    unnamed x26 -> x12, local copies, waits for them, and re-layouts: 6.56 us -> 0.78 us
    slice x1 -> x33, local copies, waits for them, and re-layouts: 0.07 us -> 2.83 us  [the longest x2 0.88 us: local(): inverse_first = got[:, 24:40].reshape(256, 128)]
    broadcast_in_dim x8, local copies, waits for them, and re-layouts: 0.29 us -> 2.54 us  [the longest x2 1.49 us: to_all(): return exchange(jnp.broadcast_to(value[None], (count, *value.shape)), axes)]
    concatenate x1 -> x14, other arithmetic: 0.62 us -> 2.77 us  [the longest x1 1.03 us: local(): jnp.concatenate([product, jnp.broadcast_to(own[None], (8, 16, 128))], axi...]
  transfers between devices with their start and end apart: 3 -> 5, of which waited for: 3 -> 5; matrix products, arithmetic and copies ran while one was open for 0% -> 0% of each run, Pallas kernels for 0% -> 0%
where the time goes in v1:
time: 122 us; the launch traced here: 121 us
  waiting for transfers between devices  42.1 us (35%)
  starting transfers between devices  33.4 us (27%)
  blocking collectives  28.1 us (23%)
  local copies, waits for them, and re-layouts  9.24 us (8%)
  other arithmetic  3.6 us (3%)
  matrix products  3.41 us (3%)
    all_to_all x5, waiting for transfers between devices, exchange(): return lax.all_to_all(value, axes, 0, 0, tiled=True)  42.1 us
    all_to_all x5, starting transfers between devices, exchange(): return lax.all_to_all(value, axes, 0, 0, tiled=True)  33.4 us
    all_to_all x1, blocking collectives, exchange(): return lax.all_to_all(value, axes, 0, 0, tiled=True)  28.1 us
    dot_general x4, matrix products, dot(): return jnp.dot(a, b, precision=HIGHEST)  2.98 us
  transfers between devices with their start and end apart: 5, of which 5 were waited for; matrix products, arithmetic and copies ran while one was open for 0% of the time, Pallas kernels for 0%

profile of v1, /device:TPU:1, one launch (start us, length us, event | category | flops | bytes accessed | tf_op | source)
XLA Modules:
  0.0 121.1 jit_solution(13161068691296100716)
XLA Ops:
  0.7 0.9 reshape.111
  1.6 0.1 broadcast_in_dim.24
  1.7 0.7 fusion.26
  2.5 0.1 copy.173
  2.6 0.1 copy.146
  2.7 0.1 copy.172
  2.8 0.1 copy.144
  3.0 0.6 copy-done.4
  3.5 2.2 %convolution_subtract_fusion = f32[32,64]{1,0:T(8,128)S(1)} fusion(f32[32,4096]{1,0:T(8,128)S(1)} %copy-done.2, f32[4096,64]{0,1:T(8,128)} %param.8, f32[32,64]{1,0:T(8,128)S(1)} %copy-done.4, pred[]{:T(512)S(6)} %eq.5), kind=kOutput, calls=%fused_computation.1 | convolution fusion | flops 100667392 | bytes 1589249 | tf_op jit(solution)/shard_map/dot_general | solution.py:11
  5.7 0.1 reshape.108
  5.8 0.1 copy.147
  6.0 0.2 copy.148
  6.2 0.7 pad_maximum_fusion.2
  6.9 10.4 %all-to-all-start = ((f32[32,7,128]{2,1,0:T(8,128)}), f32[32,7,128]{2,1,0:T(8,128)S(1)}, u32[]{:S(2)}, u32[]{:S(2)}) async-start(f32[32,7,128]{2,1,0:T(8,128)} %pad_maximum_fusion.2), calls=%async_computation | async-start | bytes 262144 | tf_op jit(solution)/shard_map/all_to_all | solution.py:15
  17.3 7.8 %all-to-all-done = f32[32,7,128]{2,1,0:T(8,128)S(1)} async-done(((f32[32,7,128]{2,1,0:T(8,128)}), f32[32,7,128]{2,1,0:T(8,128)S(1)}, u32[]{:S(2)}, u32[]{:S(2)}) %all-to-all-start) | async-done | bytes 114720 | tf_op jit(solution)/shard_map/all_to_all | solution.py:15
  25.2 0.1 reshape.115
  25.3 0.1 reshape.116
  25.4 0.2 reshape.114
  25.6 0.1 fusion.17
  25.8 0.1 squeeze.15
  25.9 0.1 reshape.113
  26.0 0.1 slice.170
  26.1 0.1 slice.167
  26.2 0.1 slice.165
  26.3 0.1 squeeze.16
  26.5 0.1 slice.175
  26.5 0.1 fusion.7
  26.6 28.1 %all_to_all.30 = f32[16,40,128]{2,1,0:T(8,128)S(1)} all-to-all(f32[16,40,128]{2,1,0:T(8,128)S(1)} %bitcast.77), channel_id=1, replica_groups=mesh['zh'=8,'zl'=2,'x'=4,'c'=8] {'zh','zl'}, dimensions={0} | all-to-all | bytes 655360 | tf_op jit(solution)/shard_map/all_to_all | solution.py:15
  54.8 0.1 fusion.15
  54.9 0.3 fusion.3
  55.2 0.1 fusion.23
  55.3 0.7 broadcast_in_dim.28
  56.0 10.0 %all-to-all-start.2 = ((f32[8,64,128]{2,1,0:T(8,128)}), f32[8,64,128]{2,1,0:T(8,128)S(1)}, u32[]{:S(2)}, u32[]{:S(2)}) async-start(f32[8,64,128]{2,1,0:T(8,128)} %broadcast_in_dim.28), calls=%async_computation.2 | async-start | bytes 524288 | tf_op jit(solution)/shard_map/all_to_all | solution.py:15
  66.1 6.5 %all-to-all-done.2 = f32[8,64,128]{2,1,0:T(8,128)S(1)} async-done(((f32[8,64,128]{2,1,0:T(8,128)}), f32[8,64,128]{2,1,0:T(8,128)S(1)}, u32[]{:S(2)}, u32[]{:S(2)}) %all-to-all-start.2) | async-done | bytes 262176 | tf_op jit(solution)/shard_map/all_to_all | solution.py:15
  72.6 0.1 fusion.22
  72.7 0.1 pad_maximum_fusion.17
  72.8 0.1 copy.161
  72.9 0.3 fusion
  73.2 0.1 fusion.21
  73.3 0.1 pad_maximum_fusion.9
  73.3 0.1 copy.162
  73.4 0.7 broadcast_in_dim.56
  74.2 3.4 %all-to-all-start.3 = ((f32[8,80,128]{2,1,0:T(8,128)}), f32[8,80,128]{2,1,0:T(8,128)S(1)}, u32[]{:S(2)}, u32[]{:S(2)}) async-start(f32[8,80,128]{2,1,0:T(8,128)} %broadcast_in_dim.56), calls=%async_computation.3 | async-start | bytes 655360 | tf_op jit(solution)/shard_map/all_to_all | solution.py:15
  77.6 6.3 %all-to-all-done.3 = f32[8,80,128]{2,1,0:T(8,128)S(1)} async-done(((f32[8,80,128]{2,1,0:T(8,128)}), f32[8,80,128]{2,1,0:T(8,128)S(1)}, u32[]{:S(2)}, u32[]{:S(2)}) %all-to-all-start.3) | async-done | bytes 327712 | tf_op jit(solution)/shard_map/all_to_all | solution.py:15
  84.0 0.1 fusion.20
  84.1 0.9 slice-done
  85.0 0.3 fusion.29
  85.3 0.1 pad_maximum_fusion.11
  85.3 0.9 broadcast_in_dim.57
  86.2 5.9 %all-to-all-start.4 = ((f32[32,32,128]{2,1,0:T(8,128)}), f32[32,32,128]{2,1,0:T(8,128)S(1)}, u32[]{:S(2)}, u32[]{:S(2)}) async-start(f32[32,32,128]{2,1,0:T(8,128)} %bitcast.25), calls=%async_computation.4 | async-start | bytes 1048576 | tf_op jit(solution)/shard_map/all_to_all | solution.py:15
  92.2 0.1 fusion.14
  92.3 11.6 %all-to-all-done.4 = f32[32,32,128]{2,1,0:T(8,128)S(1)} async-done(((f32[32,32,128]{2,1,0:T(8,128)}), f32[32,32,128]{2,1,0:T(8,128)S(1)}, u32[]{:S(2)}, u32[]{:S(2)}) %all-to-all-start.4) | async-done | bytes 524320 | tf_op jit(solution)/shard_map/all_to_all | solution.py:15
  103.9 0.1 fusion.18
  104.1 0.4 convolution_bitcast_fusion
  104.5 0.3 copy.171
  104.9 0.1 fusion.13
  105.0 0.1 pad_maximum_fusion.18
  105.0 1.0 pad_maximum_fusion
  106.1 3.6 %all-to-all-start.5 = ((f32[8,144,128]{2,1,0:T(8,128)}), f32[8,144,128]{2,1,0:T(8,128)S(1)}, u32[]{:S(2)}, u32[]{:S(2)}) async-start(f32[8,144,128]{2,1,0:T(8,128)} %pad_maximum_fusion), calls=%async_computation.5 | async-start | bytes 1179648 | tf_op jit(solution)/shard_map/all_to_all | solution.py:15
  109.7 9.9 %all-to-all-done.5 = f32[8,144,128]{2,1,0:T(8,128)S(1)} async-done(((f32[8,144,128]{2,1,0:T(8,128)}), f32[8,144,128]{2,1,0:T(8,128)S(1)}, u32[]{:S(2)}, u32[]{:S(2)}) %all-to-all-start.5) | async-done | bytes 589856 | tf_op jit(solution)/shard_map/all_to_all | solution.py:15
  119.7 0.1 fusion.27
  119.8 0.1 copy.168
  119.9 0.6 multiply_bitcast_fusion
  120.5 0.6 pad_maximum_fusion.16
  (55 shorter events, 0.7 us)
Async XLA Ops:
  0.6 103.5 %copy-start = (bf16[2048,256]{1,0:T(8,128)(2,1)S(1)}, bf16[2048,256]{1,0:T(8,128)(2,1)}, u32[]{:S(2)}) copy-start(bf16[2048,256]{1,0:T(8,128)(2,1)} %param.12) | copy-start | bytes 3145732
  0.6 2.3 %copy-start.2 = (f32[32,4096]{1,0:T(8,128)S(1)}, f32[32,4096]{1,0:T(8,128)}, u32[]{:S(2)}) copy-start(f32[32,4096]{1,0:T(8,128)} %param.7) | copy-start | bytes 1572868
  2.8 0.7 copy-start.4
  6.9 18.2 %all-to-all-start = ((f32[32,7,128]{2,1,0:T(8,128)}), f32[32,7,128]{2,1,0:T(8,128)S(1)}, u32[]{:S(2)}, u32[]{:S(2)}) async-start(f32[32,7,128]{2,1,0:T(8,128)} %pad_maximum_fusion.2), calls=%async_computation | async-start | bytes 262144 | tf_op jit(solution)/shard_map/all_to_all | solution.py:15
  54.8 22.8 %copy-start.1 = (f32[16,40,128]{2,1,0:T(8,128)}, f32[16,40,128]{2,1,0:T(8,128)S(1)}, u32[]{:S(2)}) copy-start(f32[16,40,128]{2,1,0:T(8,128)S(1)} %all_to_all.30) | copy-start | bytes 983044
  56.0 16.5 %all-to-all-start.2 = ((f32[8,64,128]{2,1,0:T(8,128)}), f32[8,64,128]{2,1,0:T(8,128)S(1)}, u32[]{:S(2)}, u32[]{:S(2)}) async-start(f32[8,64,128]{2,1,0:T(8,128)} %broadcast_in_dim.28), calls=%async_computation.2 | async-start | bytes 524288 | tf_op jit(solution)/shard_map/all_to_all | solution.py:15
  74.2 9.8 %all-to-all-start.3 = ((f32[8,80,128]{2,1,0:T(8,128)}), f32[8,80,128]{2,1,0:T(8,128)S(1)}, u32[]{:S(2)}, u32[]{:S(2)}) async-start(f32[8,80,128]{2,1,0:T(8,128)} %broadcast_in_dim.56), calls=%async_computation.3 | async-start | bytes 655360 | tf_op jit(solution)/shard_map/all_to_all | solution.py:15
  84.1 0.9 slice-start
  86.2 17.7 %all-to-all-start.4 = ((f32[32,32,128]{2,1,0:T(8,128)}), f32[32,32,128]{2,1,0:T(8,128)S(1)}, u32[]{:S(2)}, u32[]{:S(2)}) async-start(f32[32,32,128]{2,1,0:T(8,128)} %bitcast.25), calls=%async_computation.4 | async-start | bytes 1048576 | tf_op jit(solution)/shard_map/all_to_all | solution.py:15
  106.1 3.6 %copy-start.3 = (f32[256,64]{0,1:T(8,128)S(1)}, f32[256,64]{0,1:T(8,128)}, u32[]{:S(2)}) copy-start(f32[256,64]{0,1:T(8,128)} %param.13) | copy-start | bytes 196612
  106.1 13.6 %all-to-all-start.5 = ((f32[8,144,128]{2,1,0:T(8,128)}), f32[8,144,128]{2,1,0:T(8,128)S(1)}, u32[]{:S(2)}, u32[]{:S(2)}) async-start(f32[8,144,128]{2,1,0:T(8,128)} %pad_maximum_fusion), calls=%async_computation.5 | async-start | bytes 1179648 | tf_op jit(solution)/shard_map/all_to_all | solution.py:15

commit v2 on v1

--- a/solution.py
+++ b/solution.py
@@ -58,23 +58,23 @@
     turned = lax.dynamic_index_in_dim(
         got[:, :, 6].reshape(2, 2, 8, 128), c // 4, 1, keepdims=False
     )
-    turned = turned.reshape(2, 8, 4, 2, 2, 8).transpose(4, 0, 2, 1, 3, 5).reshape(2, 8, 128)
+    turned = turned.reshape(2, 8, 4, 2, 2, 8).transpose(4, 0, 2, 1, 3, 5).reshape(16, 128)
 
     common = packed(right)
     message = jnp.stack(
         [
-            jnp.concatenate([common, last_rows[8 * h : 8 * h + 8], turned[h], first_rows])
+            jnp.concatenate([common, *(m[8 * h : 8 * h + 8] for m in (last_rows, turned, first_rows))])
             for h in range(2)
         ]
     )
-    message = jnp.broadcast_to(message[None], (8, 2, 40, 128)).reshape(16, 40, 128)
+    message = jnp.broadcast_to(message[None], (8, 2, 32, 128)).reshape(16, 32, 128)
     got = exchange(message, ("zh", "zl"))
     right = unpacked(got[:, :8])
     right_first = right[:8].reshape(128, 64)
     right_last = right[8:].reshape(128, 64)
     inverse_last = got[:, 8:16].reshape(128, 128)
     couple = got[:, 16:24].reshape(128, 128)
-    inverse_first = got[:, 24:40].reshape(256, 128)
+    inverse_first = got[:, 24:32].reshape(128, 128)
 
     parts = to_all(packed(dot(inverse_last, right_last)), "c", 8)
     y_last = unpacked(parts.sum(axis=0))
@@ -86,11 +86,11 @@
     block_last = unpacked(parts[:, 64:]).reshape(2, 4, 4, 8, 64)
     block_last = block_last.transpose(2, 1, 0, 3, 4).reshape(256, 64)
 
-    terms = packed(dot(inverse_first, right_first - bent).reshape(4, 64, 64))
-    terms = jnp.broadcast_to(terms[None], (8, 4, 32, 128)).reshape(32, 32, 128)
-    parts = exchange(terms, ("x", "c")).reshape(4, 8, 32, 128)
-    block_first = unpacked(parts.sum(axis=1)).reshape(4, 4, 16, 64)
-    block_first = block_first.transpose(1, 0, 2, 3).reshape(256, 64)
+    terms = packed(dot(inverse_first, right_first - bent).reshape(4, 32, 64))
+    terms = jnp.broadcast_to(terms[None], (16, 4, 16, 128)).reshape(64, 16, 128)
+    parts = exchange(terms, ("zl", "x", "c")).reshape(2, 4, 8, 16, 128)
+    block_first = unpacked(parts.sum(axis=2)).reshape(2, 4, 4, 8, 64)
+    block_first = block_first.transpose(2, 1, 0, 3, 4).reshape(256, 64)
     block = jnp.where(c < 4, block_first, block_last)
 
     rounded = block.astype(jnp.bfloat16)

time: 122 us -> 121 us (level)
  blocking collectives: 28.1 us -> 26.8 us
    all_to_all x1, blocking collectives: 28.1 us -> 26.8 us  [exchange(): return lax.all_to_all(value, axes, 0, 0, tiled=True)]
where the time goes in v2:
time: 121 us; the launch traced here: 120 us
  waiting for transfers between devices  43 us (36%)
  starting transfers between devices  32.7 us (27%)
  blocking collectives  26.8 us (22%)
  local copies, waits for them, and re-layouts  9.21 us (8%)
  other arithmetic  3.56 us (3%)
  matrix products  3.35 us (3%)
    all_to_all x5, waiting for transfers between devices, exchange(): return lax.all_to_all(value, axes, 0, 0, tiled=True)  43 us
    all_to_all x5, starting transfers between devices, exchange(): return lax.all_to_all(value, axes, 0, 0, tiled=True)  32.7 us
    all_to_all x1, blocking collectives, exchange(): return lax.all_to_all(value, axes, 0, 0, tiled=True)  26.8 us
    dot_general x4, matrix products, dot(): return jnp.dot(a, b, precision=HIGHEST)  2.92 us
  transfers between devices with their start and end apart: 5, of which 5 were waited for; matrix products, arithmetic and copies ran while one was open for 0% of the time, Pallas kernels for 0%

profile of v2, /device:TPU:1, one launch (start us, length us, event | category | flops | bytes accessed | tf_op | source)
XLA Modules:
  0.0 119.7 jit_solution(12936835375212532690)
XLA Ops:
  0.7 0.9 reshape.107
  1.6 0.1 broadcast_in_dim.24
  1.7 0.7 fusion.29
  2.5 0.1 copy.173
  2.6 0.1 copy.146
  2.7 0.1 copy.172
  2.8 0.1 copy.144
  3.0 0.6 copy-done.4
  3.5 2.2 %convolution_subtract_fusion = f32[32,64]{1,0:T(8,128)S(1)} fusion(f32[32,4096]{1,0:T(8,128)S(1)} %copy-done.2, f32[4096,64]{0,1:T(8,128)} %param.8, f32[32,64]{1,0:T(8,128)S(1)} %copy-done.4, pred[]{:T(512)S(6)} %eq.5), kind=kOutput, calls=%fused_computation.1 | convolution fusion | flops 100667392 | bytes 1589249 | tf_op jit(solution)/shard_map/dot_general | solution.py:11
  5.7 0.1 reshape.104
  5.8 0.1 copy.147
  6.0 0.2 copy.148
  6.2 0.7 pad_maximum_fusion.2
  6.9 10.4 %all-to-all-start = ((f32[32,7,128]{2,1,0:T(8,128)}), f32[32,7,128]{2,1,0:T(8,128)S(1)}, u32[]{:S(2)}, u32[]{:S(2)}) async-start(f32[32,7,128]{2,1,0:T(8,128)} %pad_maximum_fusion.2), calls=%async_computation | async-start | bytes 262144 | tf_op jit(solution)/shard_map/all_to_all | solution.py:15
  17.3 7.8 %all-to-all-done = f32[32,7,128]{2,1,0:T(8,128)S(1)} async-done(((f32[32,7,128]{2,1,0:T(8,128)}), f32[32,7,128]{2,1,0:T(8,128)S(1)}, u32[]{:S(2)}, u32[]{:S(2)}) %all-to-all-start) | async-done | bytes 114720 | tf_op jit(solution)/shard_map/all_to_all | solution.py:15
  25.2 0.1 reshape.111
  25.3 0.1 slice.192
  25.4 0.2 reshape.110
  25.6 0.1 fusion.18
  25.7 0.1 slice.189
  25.9 0.1 reshape.109
  26.0 0.1 slice.186
  26.1 0.1 slice.183
  26.2 0.1 slice.181
  26.3 0.1 slice.198
  26.4 0.1 slice.196
  26.5 0.1 slice.194
  26.6 0.1 maximum_bitcast_fusion.1
  26.7 26.8 %all_to_all.30 = f32[16,32,128]{2,1,0:T(8,128)S(1)} all-to-all(f32[16,32,128]{2,1,0:T(8,128)S(1)} %bitcast.77), channel_id=1, replica_groups=mesh['zh'=8,'zl'=2,'x'=4,'c'=8] {'zh','zl'}, dimensions={0} | all-to-all | bytes 524288 | tf_op jit(solution)/shard_map/all_to_all | solution.py:15
  53.5 0.1 fusion.17
  53.6 0.3 fusion.5
  53.9 0.1 fusion.26
  54.0 0.7 broadcast_in_dim.28
  54.8 8.5 %all-to-all-start.2 = ((f32[8,64,128]{2,1,0:T(8,128)}), f32[8,64,128]{2,1,0:T(8,128)S(1)}, u32[]{:S(2)}, u32[]{:S(2)}) async-start(f32[8,64,128]{2,1,0:T(8,128)} %broadcast_in_dim.28), calls=%async_computation.2 | async-start | bytes 524288 | tf_op jit(solution)/shard_map/all_to_all | solution.py:15
  63.3 6.5 %all-to-all-done.2 = f32[8,64,128]{2,1,0:T(8,128)S(1)} async-done(((f32[8,64,128]{2,1,0:T(8,128)}), f32[8,64,128]{2,1,0:T(8,128)S(1)}, u32[]{:S(2)}, u32[]{:S(2)}) %all-to-all-start.2) | async-done | bytes 262176 | tf_op jit(solution)/shard_map/all_to_all | solution.py:15
  69.8 0.1 fusion.25
  69.9 0.1 pad_maximum_fusion.14
  70.0 0.1 copy.162
  70.1 0.3 fusion.2
  70.4 0.1 fusion.24
  70.5 0.1 pad_maximum_fusion.8
  70.5 0.1 copy.163
  70.6 0.8 broadcast_in_dim.56
  71.4 3.5 %all-to-all-start.3 = ((f32[8,80,128]{2,1,0:T(8,128)}), f32[8,80,128]{2,1,0:T(8,128)S(1)}, u32[]{:S(2)}, u32[]{:S(2)}) async-start(f32[8,80,128]{2,1,0:T(8,128)} %broadcast_in_dim.56), calls=%async_computation.3 | async-start | bytes 655360 | tf_op jit(solution)/shard_map/all_to_all | solution.py:15
  74.9 6.3 %all-to-all-done.3 = f32[8,80,128]{2,1,0:T(8,128)S(1)} async-done(((f32[8,80,128]{2,1,0:T(8,128)}), f32[8,80,128]{2,1,0:T(8,128)S(1)}, u32[]{:S(2)}, u32[]{:S(2)}) %all-to-all-start.3) | async-done | bytes 327712 | tf_op jit(solution)/shard_map/all_to_all | solution.py:15
  81.2 0.1 fusion.23
  81.4 0.8 slice-done
  82.2 0.2 fusion.32
  82.4 0.1 pad_maximum_fusion.11
  82.5 0.9 broadcast_in_dim.57
  83.3 6.5 %all-to-all-start.4 = ((f32[64,16,128]{2,1,0:T(8,128)}), f32[64,16,128]{2,1,0:T(8,128)S(1)}, u32[]{:S(2)}, u32[]{:S(2)}) async-start(f32[64,16,128]{2,1,0:T(8,128)} %bitcast.25), calls=%async_computation.4 | async-start | bytes 1048576 | tf_op jit(solution)/shard_map/all_to_all | solution.py:15
  89.9 0.1 fusion.16
  90.0 12.2 %all-to-all-done.4 = f32[64,16,128]{2,1,0:T(8,128)S(1)} async-done(((f32[64,16,128]{2,1,0:T(8,128)}), f32[64,16,128]{2,1,0:T(8,128)S(1)}, u32[]{:S(2)}, u32[]{:S(2)}) %all-to-all-start.4) | async-done | bytes 524320 | tf_op jit(solution)/shard_map/all_to_all | solution.py:15
  102.2 0.1 fusion.19
  102.3 0.4 convolution_bitcast_fusion
  102.8 0.3 copy.171
  103.2 0.1 pad_maximum_fusion.15
  103.3 1.0 pad_maximum_fusion
  104.3 3.8 %all-to-all-start.5 = ((f32[8,144,128]{2,1,0:T(8,128)}), f32[8,144,128]{2,1,0:T(8,128)S(1)}, u32[]{:S(2)}, u32[]{:S(2)}) async-start(f32[8,144,128]{2,1,0:T(8,128)} %pad_maximum_fusion), calls=%async_computation.5 | async-start | bytes 1179648 | tf_op jit(solution)/shard_map/all_to_all | solution.py:15
  108.1 10.2 %all-to-all-done.5 = f32[8,144,128]{2,1,0:T(8,128)S(1)} async-done(((f32[8,144,128]{2,1,0:T(8,128)}), f32[8,144,128]{2,1,0:T(8,128)S(1)}, u32[]{:S(2)}, u32[]{:S(2)}) %all-to-all-start.5) | async-done | bytes 589856 | tf_op jit(solution)/shard_map/all_to_all | solution.py:15
  118.3 0.1 fusion.30
  118.4 0.1 copy.168
  118.6 0.6 multiply_bitcast_fusion
  119.1 0.6 pad_maximum_fusion.13
  (56 shorter events, 0.7 us)
Async XLA Ops:
  0.6 101.7 %copy-start = (bf16[2048,256]{1,0:T(8,128)(2,1)S(1)}, bf16[2048,256]{1,0:T(8,128)(2,1)}, u32[]{:S(2)}) copy-start(bf16[2048,256]{1,0:T(8,128)(2,1)} %param.12) | copy-start | bytes 3145732
  0.6 2.3 %copy-start.2 = (f32[32,4096]{1,0:T(8,128)S(1)}, f32[32,4096]{1,0:T(8,128)}, u32[]{:S(2)}) copy-start(f32[32,4096]{1,0:T(8,128)} %param.7) | copy-start | bytes 1572868
  2.8 0.7 copy-start.4
  6.9 18.2 %all-to-all-start = ((f32[32,7,128]{2,1,0:T(8,128)}), f32[32,7,128]{2,1,0:T(8,128)S(1)}, u32[]{:S(2)}, u32[]{:S(2)}) async-start(f32[32,7,128]{2,1,0:T(8,128)} %pad_maximum_fusion.2), calls=%async_computation | async-start | bytes 262144 | tf_op jit(solution)/shard_map/all_to_all | solution.py:15
  53.5 21.4 %copy-start.1 = (f32[16,32,128]{2,1,0:T(8,128)}, f32[16,32,128]{2,1,0:T(8,128)S(1)}, u32[]{:S(2)}) copy-start(f32[16,32,128]{2,1,0:T(8,128)S(1)} %all_to_all.30) | copy-start | bytes 786436
  54.8 15.0 %all-to-all-start.2 = ((f32[8,64,128]{2,1,0:T(8,128)}), f32[8,64,128]{2,1,0:T(8,128)S(1)}, u32[]{:S(2)}, u32[]{:S(2)}) async-start(f32[8,64,128]{2,1,0:T(8,128)} %broadcast_in_dim.28), calls=%async_computation.2 | async-start | bytes 524288 | tf_op jit(solution)/shard_map/all_to_all | solution.py:15
  71.4 9.8 %all-to-all-start.3 = ((f32[8,80,128]{2,1,0:T(8,128)}), f32[8,80,128]{2,1,0:T(8,128)S(1)}, u32[]{:S(2)}, u32[]{:S(2)}) async-start(f32[8,80,128]{2,1,0:T(8,128)} %broadcast_in_dim.56), calls=%async_computation.3 | async-start | bytes 655360 | tf_op jit(solution)/shard_map/all_to_all | solution.py:15
  81.3 0.8 slice-start
  83.3 18.8 %all-to-all-start.4 = ((f32[64,16,128]{2,1,0:T(8,128)}), f32[64,16,128]{2,1,0:T(8,128)S(1)}, u32[]{:S(2)}, u32[]{:S(2)}) async-start(f32[64,16,128]{2,1,0:T(8,128)} %bitcast.25), calls=%async_computation.4 | async-start | bytes 1048576 | tf_op jit(solution)/shard_map/all_to_all | solution.py:15
  104.3 3.8 %copy-start.3 = (f32[256,64]{0,1:T(8,128)S(1)}, f32[256,64]{0,1:T(8,128)}, u32[]{:S(2)}) copy-start(f32[256,64]{0,1:T(8,128)} %param.13) | copy-start | bytes 196612
  104.3 14.0 %all-to-all-start.5 = ((f32[8,144,128]{2,1,0:T(8,128)}), f32[8,144,128]{2,1,0:T(8,128)S(1)}, u32[]{:S(2)}, u32[]{:S(2)}) async-start(f32[8,144,128]{2,1,0:T(8,128)} %pad_maximum_fusion), calls=%async_computation.5 | async-start | bytes 1179648 | tf_op jit(solution)/shard_map/all_to_all | solution.py:15

commit v3 on v2

v3 whole, which is shorter than its diff:
```python
import jax
import jax.numpy as jnp
from jax import lax
from jax.experimental import pallas as pl
from jax.experimental.pallas import tpu as pltpu
from jax.sharding import Mesh
from jax.sharding import PartitionSpec as P

HIGHEST = lax.Precision.HIGHEST
VMEM = pl.BlockSpec(memory_space=pltpu.VMEM)
SMEM = pl.BlockSpec(memory_space=pltpu.SMEM)
NT = (((1,), (1,)), ((), ()))


def dot(a, b):
    return jnp.dot(a, b, precision=HIGHEST, preferred_element_type=jnp.float32)


def exchange(value, axes):
    return lax.all_to_all(value, axes, 0, 0, tiled=True)


def packed(value):
    half = value.shape[-2] // 2
    return jnp.concatenate([value[..., :half, :], value[..., half:, :]], axis=-1)


def unpacked(value):
    return jnp.concatenate([value[..., :64], value[..., 64:]], axis=-2)


def call(body, out, *args, specs=None, scratch=(), limit=32 << 20):
    return pl.pallas_call(
        body,
        out_shape=out,
        in_specs=specs or [VMEM] * len(args),
        out_specs=jax.tree.map(lambda _: VMEM, out),
        scratch_shapes=scratch,
        compiler_params=pltpu.CompilerParams(vmem_limit_bytes=limit),
    )(*args)


def f32(*shape):
    return jax.ShapeDtypeStruct(shape, jnp.float32)


def two_parts(value):
    high = value.astype(jnp.bfloat16)
    low = (value - high.astype(jnp.float32)).astype(jnp.bfloat16)
    return jnp.concatenate([high, low], axis=0)


def panel_body(column, panel, solved_t, sketch, out):
    products = lax.dot_general(
        two_parts(panel[...]), two_parts(solved_t[...]), NT, preferred_element_type=jnp.float32
    )
    total = products[:32] + products[32:]
    total = total[:, :64] + total[:, 64:]
    out[...] = jnp.where(column[0] == 0, sketch[...], 0.0) - total


def last_body(got, out):
    right = unpacked(got[8:16, 0:8].reshape(64, 128))
    terms = packed(dot(got[:, 8:16].reshape(128, 128), right))
    for k in range(8):
        out[k] = terms


def bent_body(where, parts, got, out, held):
    y_last = unpacked(parts[...].sum(axis=0))
    held[...] = y_last
    bent = dot(got[:, 16:24].reshape(128, 128), y_last).reshape(8, 2, 8, 64)
    bent = jnp.concatenate([bent[:, 0].reshape(64, 64), bent[:, 1].reshape(64, 64)], axis=1)
    piece = packed(held[pl.ds(pl.multiple_of(where[0], 32), 32), :])
    for k in range(8):
        out[k, :64] = bent
        out[k, 64:] = piece


def first_body(parts, got, out):
    bent = parts[:, :64].sum(axis=0)
    right = unpacked(got[0:8, 0:8].reshape(64, 128) - bent)
    terms = dot(got[:, 24:32].reshape(128, 128), right)
    for g in range(4):
        piece = packed(terms[32 * g : 32 * g + 32])
        for k in range(16):
            out[4 * k + g] = piece


def design_body(where, first, last, design, out, held):
    for h in range(2):
        for x in range(4):
            k = 4 * h + x
            piece = first[8 * k : 8 * k + 8].sum(axis=0)
            piece = jnp.where(where[0] < 4, piece, last[k, 64:80])
            for z in range(4):
                row = 64 * z + 16 * x + 8 * h
                held[row : row + 8, :] = piece[
                    8 * (z % 2) : 8 * (z % 2) + 8, 64 * (z // 2) : 64 * (z // 2) + 64
                ]
    turned = held[...].T.astype(jnp.bfloat16)
    own = held[pl.ds(pl.multiple_of(where[1], 32), 32), :]
    own = jnp.concatenate([own[8 * k : 8 * k + 8] for k in range(4)], axis=1)
    for k in range(8):
        out[k, :64] = lax.dot_general(
            turned, design[256 * k : 256 * k + 256], NT, preferred_element_type=jnp.float32
        )
        out[k, 64:] = own


def leverage_body(where, got, prior_t, solution_rows, leverage):
    total = prior_t[...] + got[:, :64].sum(axis=0)
    leverage[...] = jnp.sum(total * total, axis=0, keepdims=True) * (1.0 / 64)
    own = got[where[0], 64:72]
    for k in range(4):
        solution_rows[8 * k : 8 * k + 8, :] = own[:, 64 * k : 64 * k + 64]


def local(panel, solved, sketch, inverses, coupling, design, prior):
    zh, zl, x, c = (lax.axis_index(name) for name in ("zh", "zl", "x", "c"))

    start = call(
        panel_body,
        f32(32, 64),
        c.reshape(1),
        panel,
        solved.T,
        sketch,
        specs=[SMEM, VMEM, VMEM, VMEM],
    )
    rows = start.reshape(8, 2, 128)

    def by_subset(block):
        return block.reshape(16, 4, 8, 4).transpose(2, 0, 1, 3).reshape(8, 2, 128)

    pieces = jnp.concatenate([rows, by_subset(inverses[1]), by_subset(inverses[0])], axis=1)
    turned = coupling.reshape(4, 4, 2, 4, 16).transpose(3, 0, 1, 2, 4).reshape(4, 1, 4, 1, 128)
    message = jnp.concatenate(
        [
            jnp.broadcast_to(pieces[None], (4, 8, 6, 128)),
            jnp.broadcast_to(turned, (4, 2, 4, 1, 128)).reshape(4, 8, 1, 128),
        ],
        axis=2,
    )
    got = exchange(message.reshape(32, 7, 128), ("x", "c")).reshape(4, 8, 7, 128)
    right = got[:, :, :2].sum(axis=1).reshape(16, 64)
    mine = lax.dynamic_index_in_dim(got, x, 0, keepdims=False)

    def joined(block):
        return block.reshape(8, 16, 2, 8).transpose(1, 2, 0, 3).reshape(16, 128)

    last_rows = joined(mine[:, 2:4])
    first_rows = joined(mine[:, 4:6])
    turned = lax.dynamic_index_in_dim(
        got[:, :, 6].reshape(2, 2, 8, 128), c // 4, 1, keepdims=False
    )
    turned = turned.reshape(2, 8, 4, 2, 2, 8).transpose(4, 0, 2, 1, 3, 5).reshape(16, 128)

    common = packed(right)
    message = jnp.stack(
        [
            jnp.concatenate([common, *(m[8 * h : 8 * h + 8] for m in (last_rows, turned, first_rows))])
            for h in range(2)
        ]
    )
    message = jnp.broadcast_to(message[None], (8, 2, 32, 128)).reshape(16, 32, 128)
    got = exchange(message, ("zh", "zl"))

    parts = exchange(call(last_body, f32(8, 64, 128), got), "c")

    last = exchange(
        call(
            bent_body,
            f32(8, 80, 128),
            (32 * (c % 4)).reshape(1),
            parts,
            got,
            specs=[SMEM, VMEM, VMEM],
            scratch=[pltpu.VMEM((128, 64), jnp.float32)],
        ),
        ("zl", "x"),
    )

    first = exchange(call(first_body, f32(64, 16, 128), last, got), ("zl", "x", "c"))

    message = call(
        design_body,
        f32(8, 72, 256),
        jnp.stack([c, 32 * (4 * zl + x)]),
        first,
        last,
        design,
        specs=[SMEM, VMEM, VMEM, VMEM],
        scratch=[pltpu.VMEM((256, 64), jnp.float32)],
    )
    got = exchange(message, "c")
    block_solution, leverage = call(
        leverage_body,
        (f32(32, 64), f32(1, 256)),
        zh.reshape(1),
        got,
        prior.T,
        specs=[SMEM, VMEM, VMEM],
    )
    return block_solution, leverage.reshape(256)


def solution(mesh):
    fine = Mesh(mesh.devices.reshape(8, 2, 4, 8), ("zh", "zl", "x", "c"))
    r = ("zh", "zl", "x")
    in_specs = (
        P(r, "c"),
        P("c", None),
        P(r, None),
        P(None, r, "c"),
        P(r, "c"),
        P(r, "c"),
        P((*r, "c"), None),
    )
    out_specs = (P(r, None), P((*r, "c")))
    return jax.shard_map(local, mesh=fine, in_specs=in_specs, out_specs=out_specs, check_vma=False)
```

time: 121 us -> 118 us (0.975)
  blocking collectives: 26.8 us -> 36.8 us
  waiting for transfers between devices: 43 us -> 36.7 us
  Pallas kernels: 0 us -> 5.67 us
  starting transfers between devices: 32.7 us -> 29.1 us
  matrix products: 3.35 us -> 0 us
  other arithmetic: 3.56 us -> 0.89 us
  local copies, waits for them, and re-layouts: 9.21 us -> 7.17 us
    all_to_all x1 -> x2, blocking collectives: 26.8 us -> 36.8 us  [exchange(): return lax.all_to_all(value, axes, 0, 0, tiled=True)]
    all_to_all x5 -> x4, waiting for transfers between devices: 43 us -> 36.7 us  [exchange(): return lax.all_to_all(value, axes, 0, 0, tiled=True)]
    pallas_call x0 -> x6, Pallas kernels: none -> 5.67 us  [call(): pl.pallas_call(body, out_shape=out, in_specs=specs or [VMEM] * len(args),...]
    unnamed x12 -> x16, local copies, waits for them, and re-layouts: 0.78 us -> 4.38 us
    all_to_all x5 -> x4, starting transfers between devices: 32.7 us -> 29.1 us  [exchange(): return lax.all_to_all(value, axes, 0, 0, tiled=True)]
    dot_general x5 -> x0, matrix products: 3.35 us -> none  [the longest x4 2.92 us: dot(): return jnp.dot(a, b, precision=HIGHEST)]
    broadcast_in_dim x4 -> x0, local copies, waits for them, and re-layouts: 2.35 us -> none  [the longest x2 1.49 us: to_all(): return exchange(jnp.broadcast_to(value[None], (count, *value.shape)), axes)]
    concatenate x11 -> x0, other arithmetic: 2.01 us -> none  [the longest x1 1.03 us: local(): jnp.concatenate([product, jnp.broadcast_to(own[None], (8, 16, 128))], axi...]
  transfers between devices with their start and end apart: 5 -> 4, of which waited for: 5 -> 4; matrix products, arithmetic and copies ran while one was open for 0% -> 0% of each run, Pallas kernels for 0% -> 0%
where the time goes in v3:
time: 118 us; the launch traced here: 117 us
  blocking collectives  36.8 us (31%)
  waiting for transfers between devices  36.7 us (31%)
  starting transfers between devices  29.1 us (25%)
  local copies, waits for them, and re-layouts  7.17 us (6%)
  Pallas kernels  5.67 us (5%)
    all_to_all x2, blocking collectives, exchange(): return lax.all_to_all(value, axes, 0, 0, tiled=True)  36.8 us
    all_to_all x4, waiting for transfers between devices, exchange(): return lax.all_to_all(value, axes, 0, 0, tiled=True)  36.7 us
    all_to_all x4, starting transfers between devices, exchange(): return lax.all_to_all(value, axes, 0, 0, tiled=True)  29.1 us
    pallas_call x6, Pallas kernels, call(): pl.pallas_call(body, out_shape=out, in_specs=specs or [VMEM] * len(args),...  5.67 us
    unnamed x16, local copies, waits for them, and re-layouts  4.38 us
  transfers between devices with their start and end apart: 4, of which 4 were waited for; matrix products, arithmetic and copies ran while one was open for 0% of the time, Pallas kernels for 0%

profile of v3, /device:TPU:1, one launch (start us, length us, event | category | flops | bytes accessed | tf_op | source)
XLA Modules:
  0.0 117.2 jit_solution(10309230540345850442)
XLA Ops:
  0.6 0.0 copy-start
  0.6 1.2 %copy-done = f32[4096,64]{0,1:T(8,128)S(1)} copy-done((f32[4096,64]{0,1:T(8,128)S(1)}, f32[4096,64]{0,1:T(8,128)}, u32[]{:S(2)}) %copy-start) | copy-done | bytes 1048600
  1.9 0.0 copy-start.2
  1.9 1.0 copy-done.2
  2.9 0.0 copy-start.4
  2.9 0.7 copy-done.4
  3.6 0.5 shard_map.86
  4.2 0.0 copy-start.5
  4.2 0.1 reshape.69
  4.3 0.6 copy-done.5
  4.9 0.1 copy.117
  5.0 0.1 copy.100
  5.1 0.1 copy.118
  5.2 0.0 copy-start.6
  5.3 0.1 copy.102
  5.4 0.5 copy-done.6
  5.9 0.1 reshape.72
  6.1 0.1 broadcast_in_dim.22
  6.2 0.1 copy.103
  6.4 0.2 copy.104
  6.6 0.7 pad_maximum_fusion.1
  7.3 10.4 %all-to-all-start = ((f32[32,7,128]{2,1,0:T(8,128)}), f32[32,7,128]{2,1,0:T(8,128)S(1)}, u32[]{:S(2)}, u32[]{:S(2)}) async-start(f32[32,7,128]{2,1,0:T(8,128)} %pad_maximum_fusion.1), calls=%async_computation | async-start | bytes 262144 | tf_op jit(solution)/shard_map/all_to_all | solution.py:20
  17.7 7.8 %all-to-all-done = f32[32,7,128]{2,1,0:T(8,128)S(1)} async-done(((f32[32,7,128]{2,1,0:T(8,128)}), f32[32,7,128]{2,1,0:T(8,128)S(1)}, u32[]{:S(2)}, u32[]{:S(2)}) %all-to-all-start) | async-done | bytes 114720 | tf_op jit(solution)/shard_map/all_to_all | solution.py:20
  25.6 0.1 slice.70
  25.6 0.1 slice.72
  25.7 0.2 reshape.76
  26.0 0.1 slice.81
  26.2 0.1 slice.87
  26.3 0.2 reshape.75
  26.5 0.1 fusion.5
  26.6 0.1 slice.78
  26.8 0.1 slice.85
  26.9 0.2 reshape.74
  27.2 0.1 slice.75
  27.4 0.1 slice.83
  27.5 0.1 maximum_bitcast_fusion
  27.6 26.8 %all_to_all.30.got = f32[16,32,128]{2,1,0:T(8,128)S(1)} all-to-all(f32[16,32,128]{2,1,0:T(8,128)S(1)} %bitcast.46), channel_id=1, replica_groups=mesh['zh'=8,'zl'=2,'x'=4,'c'=8] {'zh','zl'}, dimensions={0} | all-to-all | bytes 524288 | tf_op jit(solution)/shard_map/all_to_all | solution.py:20
  54.3 1.0 shard_map.87
  55.4 8.5 %all-to-all-start.2 = ((f32[8,64,128]{2,1,0:T(8,128)}), f32[8,64,128]{2,1,0:T(8,128)S(1)}, u32[]{:S(2)}, u32[]{:S(2)}) async-start(f32[8,64,128]{2,1,0:T(8,128)} %shard_map.87), calls=%async_computation.2 | async-start | bytes 524288 | tf_op jit(solution)/shard_map/all_to_all | solution.py:20
  63.9 6.5 %all-to-all-done.2.parts = f32[8,64,128]{2,1,0:T(8,128)S(1)} async-done(((f32[8,64,128]{2,1,0:T(8,128)}), f32[8,64,128]{2,1,0:T(8,128)S(1)}, u32[]{:S(2)}, u32[]{:S(2)}) %all-to-all-start.2) | async-done | bytes 262176 | tf_op jit(solution)/shard_map/all_to_all | solution.py:20
  70.4 0.3 shard_map.88
  70.8 10.0 %all_to_all.31.parts.last = f32[8,80,128]{2,1,0:T(8,128)S(1)} all-to-all(f32[8,80,128]{2,1,0:T(8,128)S(1)} %shard_map.88), channel_id=1, replica_groups=mesh['zh'=8,'zl'=2,'x'=4,'c'=8] {'zl','x'}, dimensions={0} | all-to-all | bytes 655360 | tf_op jit(solution)/shard_map/all_to_all | solution.py:20
  80.7 0.0 copy-start.1
  80.7 1.2 shard_map.89
  81.9 6.4 %all-to-all-start.4 = ((f32[64,16,128]{2,1,0:T(8,128)}), f32[64,16,128]{2,1,0:T(8,128)S(1)}, u32[]{:S(2)}, u32[]{:S(2)}) async-start(f32[64,16,128]{2,1,0:T(8,128)} %shard_map.89), calls=%async_computation.4 | async-start | bytes 1048576 | tf_op jit(solution)/shard_map/all_to_all | solution.py:20
  88.4 0.1 pad_add_fusion.where
  88.5 12.2 %all-to-all-done.4.first = f32[64,16,128]{2,1,0:T(8,128)S(1)} async-done(((f32[64,16,128]{2,1,0:T(8,128)}), f32[64,16,128]{2,1,0:T(8,128)S(1)}, u32[]{:S(2)}, u32[]{:S(2)}) %all-to-all-start.4) | async-done | bytes 524320 | tf_op jit(solution)/shard_map/all_to_all | solution.py:20
  100.7 0.0 copy-done.1
  100.7 1.9 %shard_map.90 = f32[8,72,256]{2,1,0:T(8,128)} custom-call(s32[2]{0:T(128)S(1)} %pad_add_fusion.where, f32[64,16,128]{2,1,0:T(8,128)S(1)} %all-to-all-done.4.first, f32[8,80,128]{2,1,0:T(8,128)S(1)} %all_to_all.31.parts.last, bf16[2048,256]{1,0:T(8,128)(2,1)S(1)} %copy-done.1), custom_call_target="tpu_custom_call" | custom-call | tf_op jit(solution)/shard_map/pallas_call | solution.py:33
  102.6 0.0 copy-start.3
  102.6 3.8 %all-to-all-start.5 = ((f32[8,72,256]{2,1,0:T(8,128)}), f32[8,72,256]{2,1,0:T(8,128)S(1)}, u32[]{:S(2)}, u32[]{:S(2)}) async-start(f32[8,72,256]{2,1,0:T(8,128)} %shard_map.90), calls=%async_computation.5 | async-start | bytes 1179648 | tf_op jit(solution)/shard_map/all_to_all | solution.py:20
  106.4 10.2 %all-to-all-done.5.got = f32[8,72,256]{2,1,0:T(8,128)S(1)} async-done(((f32[8,72,256]{2,1,0:T(8,128)}), f32[8,72,256]{2,1,0:T(8,128)S(1)}, u32[]{:S(2)}, u32[]{:S(2)}) %all-to-all-start.5) | async-done | bytes 589856 | tf_op jit(solution)/shard_map/all_to_all | solution.py:20
  116.6 0.0 copy-done.3
  116.6 0.7 shard_map.91
  (26 shorter events, 0.4 us)
Async XLA Ops:
  0.6 1.2 %copy-start = (f32[4096,64]{0,1:T(8,128)S(1)}, f32[4096,64]{0,1:T(8,128)}, u32[]{:S(2)}) copy-start(f32[4096,64]{0,1:T(8,128)} %param.8) | copy-start | bytes 3145732
  1.9 1.0 copy-start.2
  2.9 0.7 copy-start.4
  4.2 0.7 copy-start.5
  5.2 0.7 copy-start.6
  7.3 18.2 %all-to-all-start = ((f32[32,7,128]{2,1,0:T(8,128)}), f32[32,7,128]{2,1,0:T(8,128)S(1)}, u32[]{:S(2)}, u32[]{:S(2)}) async-start(f32[32,7,128]{2,1,0:T(8,128)} %pad_maximum_fusion.1), calls=%async_computation | async-start | bytes 262144 | tf_op jit(solution)/shard_map/all_to_all | solution.py:20
  55.4 15.0 %all-to-all-start.2 = ((f32[8,64,128]{2,1,0:T(8,128)}), f32[8,64,128]{2,1,0:T(8,128)S(1)}, u32[]{:S(2)}, u32[]{:S(2)}) async-start(f32[8,64,128]{2,1,0:T(8,128)} %shard_map.87), calls=%async_computation.2 | async-start | bytes 524288 | tf_op jit(solution)/shard_map/all_to_all | solution.py:20
  80.7 19.9 %copy-start.1 = (bf16[2048,256]{1,0:T(8,128)(2,1)S(1)}, bf16[2048,256]{1,0:T(8,128)(2,1)}, u32[]{:S(2)}) copy-start(bf16[2048,256]{1,0:T(8,128)(2,1)} %design.1) | copy-start | bytes 3145732
  81.9 18.7 %all-to-all-start.4 = ((f32[64,16,128]{2,1,0:T(8,128)}), f32[64,16,128]{2,1,0:T(8,128)S(1)}, u32[]{:S(2)}, u32[]{:S(2)}) async-start(f32[64,16,128]{2,1,0:T(8,128)} %shard_map.89), calls=%async_computation.4 | async-start | bytes 1048576 | tf_op jit(solution)/shard_map/all_to_all | solution.py:20
  102.6 14.0 %copy-start.3 = (f32[256,64]{0,1:T(8,128)S(1)}, f32[256,64]{0,1:T(8,128)}, u32[]{:S(2)}) copy-start(f32[256,64]{0,1:T(8,128)} %param.13) | copy-start | bytes 196612
  102.6 14.0 %all-to-all-start.5 = ((f32[8,72,256]{2,1,0:T(8,128)}), f32[8,72,256]{2,1,0:T(8,128)S(1)}, u32[]{:S(2)}, u32[]{:S(2)}) async-start(f32[8,72,256]{2,1,0:T(8,128)} %shard_map.90), calls=%async_computation.5 | async-start | bytes 1179648 | tf_op jit(solution)/shard_map/all_to_all | solution.py:20

commit v4 on v3

--- a/solution.py
+++ b/solution.py
@@ -50,17 +50,110 @@
     return jnp.concatenate([high, low], axis=0)
 
 
-def panel_body(column, panel, solved_t, sketch, out):
+def permuted(value, source_of):
+    row = lax.broadcasted_iota(jnp.int32, (128, 128), 0)
+    lane = lax.broadcasted_iota(jnp.int32, (128, 128), 1)
+    return dot(value, (row == source_of(lane)).astype(jnp.float32))
+
+
+def staggered(value, step, shift=0):
+    row = lax.broadcasted_iota(jnp.int32, value.shape, 0) % (128 // (step % 128 & -(step % 128)))
+    out = value
+    for i in range(128 // (step % 128 & -(step % 128))):
+        turn = (shift + step * i) % 128
+        out = jnp.where(row == i, pltpu.roll(value, turn, 1) if turn else value, out)
+    return out
+
+
+def start_body(column, panel_hbm, solved_hbm, sketch_hbm, inverses_hbm, coupling_hbm, out, *held):
+    sources = (inverses_hbm, coupling_hbm, panel_hbm, solved_hbm, sketch_hbm)
+    inverses, coupling, panel, solved_t, sketch, sems = held
+    copies = [
+        pltpu.make_async_copy(source, target, sems.at[k])
+        for k, (source, target) in enumerate(zip(sources, held))
+    ]
+    for copy in copies:
+        copy.start()
+
+    copies[0].wait()
+    both = jnp.concatenate([inverses[1], inverses[0]], axis=0)
+    both = permuted(both, lambda m: 32 * (m % 16 // 4) + 4 * (m // 16) + m % 4)
+    both = staggered(both, 16)
+    group = lax.broadcasted_iota(jnp.int32, (32, 128), 1) // 16
+    row = lax.broadcasted_iota(jnp.int32, (32, 128), 0)
+    for c2 in range(8):
+        kept = jnp.where(group == (c2 + row) % 8, both, 0.0)
+        kept = kept.reshape(4, 8, 128).sum(axis=1)
+        for x2 in range(4):
+            out[8 * x2 + c2, 2:6] = kept
+
+    copies[1].wait()
+    couple = permuted(
+        coupling[...], lambda m: 64 * (m % 16 // 8) + 16 * (m // 32) + 8 * (m % 32 // 16) + m % 8
+    )
+    couple = staggered(couple, 32)
+    group = group[:16] // 2
+    row = row[:16]
+    for x2 in range(4):
+        kept = jnp.where(group == (x2 + row) % 4, couple, 0.0)
+        for g in range(4):
+            piece = jnp.sum(jnp.where(row // 4 == g, kept, 0.0), axis=0, keepdims=True)
+            out[8 * x2 + g, 6:7] = piece
+            out[8 * x2 + 4 + g, 6:7] = piece
+            out[8 * x2 + g, 7:8] = piece
+            out[8 * x2 + 4 + g, 7:8] = piece
+
+    for copy in copies[2:]:
+        copy.wait()
     products = lax.dot_general(
         two_parts(panel[...]), two_parts(solved_t[...]), NT, preferred_element_type=jnp.float32
     )
     total = products[:32] + products[32:]
     total = total[:, :64] + total[:, 64:]
-    out[...] = jnp.where(column[0] == 0, sketch[...], 0.0) - total
+    total = jnp.where(column[0] == 0, sketch[...], 0.0) - total
+    for c2 in range(8):
+        piece = packed(total[4 * c2 : 4 * c2 + 4])
+        for x2 in range(4):
+            out[8 * x2 + c2, 0:2] = piece
+
+
+def split_body(where, got, out):
+    x, c = where[0], where[1]
+    right = [unpacked(got[8 * k : 8 * k + 8, 0:2].sum(axis=0)) for k in range(4)]
+    right = jnp.concatenate(
+        [jnp.concatenate(right[:2], axis=0), jnp.concatenate(right[2:], axis=0)], axis=1
+    )
+    group = lax.broadcasted_iota(jnp.int32, (8, 128), 1) // 16
+    row = lax.broadcasted_iota(jnp.int32, (8, 128), 0)
+
+    mats = [jnp.zeros((8, 128), jnp.float32) for _ in range(4)]
+    for c1 in range(8):
+        piece = got[8 * x + c1, 2:6]
+        piece = pltpu.roll(piece, (16 * (c1 + 8) - 16 * c) % 128, 1)
+        for k in range(4):
+            mats[k] = jnp.where(group == (c1 + row) % 8, piece[k : k + 1], mats[k])
+    mats = [staggered(mat, -16) for mat in mats]
+
+    halves = [jnp.zeros((8, 128), jnp.float32) for _ in range(2)]
+    for a in range(2):
+        for c1 in range(8):
+            piece = got[8 * (c // 4 + 2 * a) + c1, 6:8]
+            piece = pltpu.roll(piece, (16 * c1 + 128 - 32 * x) % 128, 1)[:1]
+            for h in range(2):
+                here = (group == (2 * row + h + c1) % 8) & (row // 4 == a)
+                halves[h] = jnp.where(here, piece, halves[h])
+    halves = [staggered(half, -32, -16 * h) for h, half in enumerate(halves)]
+
+    for k in range(8):
+        for h in range(2):
+            out[2 * k + h, 0:8] = right
+            out[2 * k + h, 8:16] = mats[h]
+            out[2 * k + h, 16:24] = halves[h]
+            out[2 * k + h, 24:32] = mats[2 + h]
 
 
 def last_body(got, out):
-    right = unpacked(got[8:16, 0:8].reshape(64, 128))
+    right = unpacked(got[8:16, 0:8]).reshape(128, 64)
     terms = packed(dot(got[:, 8:16].reshape(128, 128), right))
     for k in range(8):
         out[k] = terms
@@ -79,7 +172,7 @@
 
 def first_body(parts, got, out):
     bent = parts[:, :64].sum(axis=0)
-    right = unpacked(got[0:8, 0:8].reshape(64, 128) - bent)
+    right = unpacked(got[0:8, 0:8] - bent.reshape(8, 8, 128)).reshape(128, 64)
     terms = dot(got[:, 24:32].reshape(128, 128), right)
     for g in range(4):
         piece = packed(terms[32 * g : 32 * g + 32])
@@ -119,51 +212,28 @@
 def local(panel, solved, sketch, inverses, coupling, design, prior):
     zh, zl, x, c = (lax.axis_index(name) for name in ("zh", "zl", "x", "c"))
 
-    start = call(
-        panel_body,
-        f32(32, 64),
+    message = call(
+        start_body,
+        f32(32, 8, 128),
         c.reshape(1),
         panel,
         solved.T,
         sketch,
-        specs=[SMEM, VMEM, VMEM, VMEM],
-    )
-    rows = start.reshape(8, 2, 128)
-
-    def by_subset(block):
-        return block.reshape(16, 4, 8, 4).transpose(2, 0, 1, 3).reshape(8, 2, 128)
-
-    pieces = jnp.concatenate([rows, by_subset(inverses[1]), by_subset(inverses[0])], axis=1)
-    turned = coupling.reshape(4, 4, 2, 4, 16).transpose(3, 0, 1, 2, 4).reshape(4, 1, 4, 1, 128)
-    message = jnp.concatenate(
-        [
-            jnp.broadcast_to(pieces[None], (4, 8, 6, 128)),
-            jnp.broadcast_to(turned, (4, 2, 4, 1, 128)).reshape(4, 8, 1, 128),
+        inverses,
+        coupling,
+        specs=[SMEM] + [pl.BlockSpec(memory_space=pl.ANY)] * 5,
+        scratch=[
+            pltpu.VMEM((2, 16, 128), jnp.float32),
+            pltpu.VMEM((16, 128), jnp.float32),
+            pltpu.VMEM((32, 4096), jnp.float32),
+            pltpu.VMEM((64, 4096), jnp.float32),
+            pltpu.VMEM((32, 64), jnp.float32),
+            pltpu.SemaphoreType.DMA((5,)),
         ],
-        axis=2,
-    )
-    got = exchange(message.reshape(32, 7, 128), ("x", "c")).reshape(4, 8, 7, 128)
-    right = got[:, :, :2].sum(axis=1).reshape(16, 64)
-    mine = lax.dynamic_index_in_dim(got, x, 0, keepdims=False)
-
-    def joined(block):
-        return block.reshape(8, 16, 2, 8).transpose(1, 2, 0, 3).reshape(16, 128)
-
-    last_rows = joined(mine[:, 2:4])
-    first_rows = joined(mine[:, 4:6])
-    turned = lax.dynamic_index_in_dim(
-        got[:, :, 6].reshape(2, 2, 8, 128), c // 4, 1, keepdims=False
-    )
-    turned = turned.reshape(2, 8, 4, 2, 2, 8).transpose(4, 0, 2, 1, 3, 5).reshape(16, 128)
-
-    common = packed(right)
-    message = jnp.stack(
-        [
-            jnp.concatenate([common, *(m[8 * h : 8 * h + 8] for m in (last_rows, turned, first_rows))])
-            for h in range(2)
-        ]
-    )
-    message = jnp.broadcast_to(message[None], (8, 2, 32, 128)).reshape(16, 32, 128)
+    )
+    got = exchange(message, ("x", "c"))
+
+    message = call(split_body, f32(16, 32, 128), jnp.stack([x, c]), got, specs=[SMEM, VMEM])
     got = exchange(message, ("zh", "zl"))
 
     parts = exchange(call(last_body, f32(8, 64, 128), got), "c")

time: 118 us -> 117 us (level)
  local copies, waits for them, and re-layouts: 7.17 us -> 4.39 us
  Pallas kernels: 5.67 us -> 8.05 us
    pallas_call x6 -> x7, Pallas kernels: 5.67 us -> 8.05 us  [call(): pl.pallas_call(body, out_shape=out, in_specs=specs or [VMEM] * len(args),...]
    unnamed x16 -> x14, local copies, waits for them, and re-layouts: 4.38 us -> 4.39 us
where the time goes in v4:
time: 117 us; the launch traced here: 116 us
  blocking collectives  36.8 us (31%)
  waiting for transfers between devices  36.7 us (31%)
  starting transfers between devices  29.1 us (25%)
  Pallas kernels  8.05 us (7%)
  local copies, waits for them, and re-layouts  4.39 us (4%)
    all_to_all x2, blocking collectives, exchange(): return lax.all_to_all(value, axes, 0, 0, tiled=True)  36.8 us
    all_to_all x4, waiting for transfers between devices, exchange(): return lax.all_to_all(value, axes, 0, 0, tiled=True)  36.7 us
    all_to_all x4, starting transfers between devices, exchange(): return lax.all_to_all(value, axes, 0, 0, tiled=True)  29.1 us
    pallas_call x7, Pallas kernels, call(): pl.pallas_call(body, out_shape=out, in_specs=specs or [VMEM] * len(args),...  8.05 us
    unnamed x14, local copies, waits for them, and re-layouts  4.39 us
  transfers between devices with their start and end apart: 4, of which 4 were waited for; matrix products, arithmetic and copies ran while one was open for 0% of the time, Pallas kernels for 0%

profile of v4, /device:TPU:1, one launch (start us, length us, event | category | flops | bytes accessed | tf_op | source)
XLA Modules:
  0.0 115.8 jit_solution(5171866248904448233)
XLA Ops:
  0.6 0.0 copy-start.6
  0.6 0.7 copy-done.6
  1.3 0.0 copy-start
  1.3 1.2 %copy-done = f32[4096,64]{0,1:T(8,128)S(1)} copy-done((f32[4096,64]{0,1:T(8,128)S(1)}, f32[4096,64]{0,1:T(8,128)}, u32[]{:S(2)}) %copy-start) | copy-done | bytes 1048600
  2.6 0.0 copy-start.2
  2.6 1.0 copy-done.2
  3.6 0.0 copy-start.4
  3.6 0.7 copy-done.4
  4.3 0.0 copy-start.5
  4.3 0.7 copy-done.5
  5.0 2.1 %shard_map.86 = f32[32,8,128]{2,1,0:T(8,128)} custom-call(s32[1]{0:T(128)} %bitcast.1.column, f32[32,4096]{1,0:T(8,128)S(1)} %copy-done.2, f32[64,4096]{1,0:T(8,128)S(1)} %bitcast.8, f32[32,64]{1,0:T(8,128)S(1)} %copy-done.4, f32[2,16,128]{2,1,0:T(8,128)S(1)} %copy-done.5, f32[16,128]{1,0:T(8,128)S(1)} %copy-done.6), custom_call_target="tpu_custom_call" | custom-call | tf_op jit(solution)/shard_map/pallas_call | solution.py:33
  7.2 10.4 %all-to-all-start = ((f32[32,8,128]{2,1,0:T(8,128)}), f32[32,8,128]{2,1,0:T(8,128)S(1)}, u32[]{:S(2)}, u32[]{:S(2)}) async-start(f32[32,8,128]{2,1,0:T(8,128)} %shard_map.86), calls=%async_computation | async-start | bytes 262144 | tf_op jit(solution)/shard_map/all_to_all | solution.py:20
  17.6 0.1 pad_add_fusion.1.where
  17.7 7.7 %all-to-all-done.got = f32[32,8,128]{2,1,0:T(8,128)S(1)} async-done(((f32[32,8,128]{2,1,0:T(8,128)}), f32[32,8,128]{2,1,0:T(8,128)S(1)}, u32[]{:S(2)}, u32[]{:S(2)}) %all-to-all-start) | async-done | bytes 131104 | tf_op jit(solution)/shard_map/all_to_all | solution.py:20
  25.4 0.8 shard_map.87
  26.2 26.8 %all_to_all.30.got = f32[16,32,128]{2,1,0:T(8,128)S(1)} all-to-all(f32[16,32,128]{2,1,0:T(8,128)S(1)} %shard_map.87), channel_id=1, replica_groups=mesh['zh'=8,'zl'=2,'x'=4,'c'=8] {'zh','zl'}, dimensions={0} | all-to-all | bytes 524288 | tf_op jit(solution)/shard_map/all_to_all | solution.py:20
  53.0 1.0 shard_map.88
  54.0 8.5 %all-to-all-start.2 = ((f32[8,64,128]{2,1,0:T(8,128)}), f32[8,64,128]{2,1,0:T(8,128)S(1)}, u32[]{:S(2)}, u32[]{:S(2)}) async-start(f32[8,64,128]{2,1,0:T(8,128)} %shard_map.88), calls=%async_computation.2 | async-start | bytes 524288 | tf_op jit(solution)/shard_map/all_to_all | solution.py:20
  62.5 6.5 %all-to-all-done.2.parts = f32[8,64,128]{2,1,0:T(8,128)S(1)} async-done(((f32[8,64,128]{2,1,0:T(8,128)}), f32[8,64,128]{2,1,0:T(8,128)S(1)}, u32[]{:S(2)}, u32[]{:S(2)}) %all-to-all-start.2) | async-done | bytes 262176 | tf_op jit(solution)/shard_map/all_to_all | solution.py:20
  69.0 0.3 shard_map.89
  69.4 10.0 %all_to_all.31.parts.last = f32[8,80,128]{2,1,0:T(8,128)S(1)} all-to-all(f32[8,80,128]{2,1,0:T(8,128)S(1)} %shard_map.89), channel_id=1, replica_groups=mesh['zh'=8,'zl'=2,'x'=4,'c'=8] {'zl','x'}, dimensions={0} | all-to-all | bytes 655360 | tf_op jit(solution)/shard_map/all_to_all | solution.py:20
  79.4 0.0 copy-start.1
  79.4 1.2 %shard_map.90 = f32[64,16,128]{2,1,0:T(8,128)} custom-call(f32[8,80,128]{2,1,0:T(8,128)S(1)} %all_to_all.31.parts.last, f32[16,32,128]{2,1,0:T(8,128)S(1)} %all_to_all.30.got), custom_call_target="tpu_custom_call" | custom-call | tf_op jit(solution)/shard_map/pallas_call | solution.py:33
  80.5 6.4 %all-to-all-start.4 = ((f32[64,16,128]{2,1,0:T(8,128)}), f32[64,16,128]{2,1,0:T(8,128)S(1)}, u32[]{:S(2)}, u32[]{:S(2)}) async-start(f32[64,16,128]{2,1,0:T(8,128)} %shard_map.90), calls=%async_computation.4 | async-start | bytes 1048576 | tf_op jit(solution)/shard_map/all_to_all | solution.py:20
  87.0 0.1 pad_add_fusion.where
  87.1 12.2 %all-to-all-done.4.first = f32[64,16,128]{2,1,0:T(8,128)S(1)} async-done(((f32[64,16,128]{2,1,0:T(8,128)}), f32[64,16,128]{2,1,0:T(8,128)S(1)}, u32[]{:S(2)}, u32[]{:S(2)}) %all-to-all-start.4) | async-done | bytes 524320 | tf_op jit(solution)/shard_map/all_to_all | solution.py:20
  99.3 0.0 copy-done.1
  99.3 1.9 %shard_map.91 = f32[8,72,256]{2,1,0:T(8,128)} custom-call(s32[2]{0:T(128)S(1)} %pad_add_fusion.where, f32[64,16,128]{2,1,0:T(8,128)S(1)} %all-to-all-done.4.first, f32[8,80,128]{2,1,0:T(8,128)S(1)} %all_to_all.31.parts.last, bf16[2048,256]{1,0:T(8,128)(2,1)S(1)} %copy-done.1), custom_call_target="tpu_custom_call" | custom-call | tf_op jit(solution)/shard_map/pallas_call | solution.py:33
  101.2 0.0 copy-start.3
  101.2 3.8 %all-to-all-start.5 = ((f32[8,72,256]{2,1,0:T(8,128)}), f32[8,72,256]{2,1,0:T(8,128)S(1)}, u32[]{:S(2)}, u32[]{:S(2)}) async-start(f32[8,72,256]{2,1,0:T(8,128)} %shard_map.91), calls=%async_computation.5 | async-start | bytes 1179648 | tf_op jit(solution)/shard_map/all_to_all | solution.py:20
  105.0 10.2 %all-to-all-done.5.got = f32[8,72,256]{2,1,0:T(8,128)S(1)} async-done(((f32[8,72,256]{2,1,0:T(8,128)}), f32[8,72,256]{2,1,0:T(8,128)S(1)}, u32[]{:S(2)}, u32[]{:S(2)}) %all-to-all-start.5) | async-done | bytes 589856 | tf_op jit(solution)/shard_map/all_to_all | solution.py:20
  115.2 0.0 copy-done.3
  115.2 0.7 shard_map.92
Async XLA Ops:
  0.6 0.7 copy-start.6
  1.3 1.2 %copy-start = (f32[4096,64]{0,1:T(8,128)S(1)}, f32[4096,64]{0,1:T(8,128)}, u32[]{:S(2)}) copy-start(f32[4096,64]{0,1:T(8,128)} %param.8) | copy-start | bytes 3145732
  2.6 1.0 copy-start.2
  3.6 0.7 copy-start.4
  4.3 0.7 copy-start.5
  7.2 18.2 %all-to-all-start = ((f32[32,8,128]{2,1,0:T(8,128)}), f32[32,8,128]{2,1,0:T(8,128)S(1)}, u32[]{:S(2)}, u32[]{:S(2)}) async-start(f32[32,8,128]{2,1,0:T(8,128)} %shard_map.86), calls=%async_computation | async-start | bytes 262144 | tf_op jit(solution)/shard_map/all_to_all | solution.py:20
  54.0 15.0 %all-to-all-start.2 = ((f32[8,64,128]{2,1,0:T(8,128)}), f32[8,64,128]{2,1,0:T(8,128)S(1)}, u32[]{:S(2)}, u32[]{:S(2)}) async-start(f32[8,64,128]{2,1,0:T(8,128)} %shard_map.88), calls=%async_computation.2 | async-start | bytes 524288 | tf_op jit(solution)/shard_map/all_to_all | solution.py:20
  79.4 19.9 %copy-start.1 = (bf16[2048,256]{1,0:T(8,128)(2,1)S(1)}, bf16[2048,256]{1,0:T(8,128)(2,1)}, u32[]{:S(2)}) copy-start(bf16[2048,256]{1,0:T(8,128)(2,1)} %design.1) | copy-start | bytes 3145732
  80.5 18.7 %all-to-all-start.4 = ((f32[64,16,128]{2,1,0:T(8,128)}), f32[64,16,128]{2,1,0:T(8,128)S(1)}, u32[]{:S(2)}, u32[]{:S(2)}) async-start(f32[64,16,128]{2,1,0:T(8,128)} %shard_map.90), calls=%async_computation.4 | async-start | bytes 1048576 | tf_op jit(solution)/shard_map/all_to_all | solution.py:20
  101.2 14.0 %copy-start.3 = (f32[256,64]{0,1:T(8,128)S(1)}, f32[256,64]{0,1:T(8,128)}, u32[]{:S(2)}) copy-start(f32[256,64]{0,1:T(8,128)} %param.13) | copy-start | bytes 196612
  101.2 14.0 %all-to-all-start.5 = ((f32[8,72,256]{2,1,0:T(8,128)}), f32[8,72,256]{2,1,0:T(8,128)S(1)}, u32[]{:S(2)}, u32[]{:S(2)}) async-start(f32[8,72,256]{2,1,0:T(8,128)} %shard_map.91), calls=%async_computation.5 | async-start | bytes 1179648 | tf_op jit(solution)/shard_map/all_to_all | solution.py:20

commit v5 on v4

--- a/solution.py
+++ b/solution.py
@@ -65,7 +65,7 @@
     return out
 
 
-def start_body(column, panel_hbm, solved_hbm, sketch_hbm, inverses_hbm, coupling_hbm, out, *held):
+def start_body(where, panel_hbm, solved_hbm, sketch_hbm, inverses_hbm, coupling_hbm, out, *held):
     sources = (inverses_hbm, coupling_hbm, panel_hbm, solved_hbm, sketch_hbm)
     inverses, coupling, panel, solved_t, sketch, sems = held
     copies = [
@@ -110,7 +110,7 @@
     )
     total = products[:32] + products[32:]
     total = total[:, :64] + total[:, 64:]
-    total = jnp.where(column[0] == 0, sketch[...], 0.0) - total
+    total = jnp.where(where[1] == 0, sketch[...], 0.0) - total
     for c2 in range(8):
         piece = packed(total[4 * c2 : 4 * c2 + 4])
         for x2 in range(4):
@@ -164,7 +164,7 @@
     held[...] = y_last
     bent = dot(got[:, 16:24].reshape(128, 128), y_last).reshape(8, 2, 8, 64)
     bent = jnp.concatenate([bent[:, 0].reshape(64, 64), bent[:, 1].reshape(64, 64)], axis=1)
-    piece = packed(held[pl.ds(pl.multiple_of(where[0], 32), 32), :])
+    piece = packed(held[pl.ds(pl.multiple_of(where[3], 32), 32), :])
     for k in range(8):
         out[k, :64] = bent
         out[k, 64:] = piece
@@ -185,14 +185,14 @@
         for x in range(4):
             k = 4 * h + x
             piece = first[8 * k : 8 * k + 8].sum(axis=0)
-            piece = jnp.where(where[0] < 4, piece, last[k, 64:80])
+            piece = jnp.where(where[1] < 4, piece, last[k, 64:80])
             for z in range(4):
                 row = 64 * z + 16 * x + 8 * h
                 held[row : row + 8, :] = piece[
                     8 * (z % 2) : 8 * (z % 2) + 8, 64 * (z // 2) : 64 * (z // 2) + 64
                 ]
     turned = held[...].T.astype(jnp.bfloat16)
-    own = held[pl.ds(pl.multiple_of(where[1], 32), 32), :]
+    own = held[pl.ds(pl.multiple_of(where[4], 32), 32), :]
     own = jnp.concatenate([own[8 * k : 8 * k + 8] for k in range(4)], axis=1)
     for k in range(8):
         out[k, :64] = lax.dot_general(
@@ -204,18 +204,20 @@
 def leverage_body(where, got, prior_t, solution_rows, leverage):
     total = prior_t[...] + got[:, :64].sum(axis=0)
     leverage[...] = jnp.sum(total * total, axis=0, keepdims=True) * (1.0 / 64)
-    own = got[where[0], 64:72]
+    own = got[where[2], 64:72]
     for k in range(4):
         solution_rows[8 * k : 8 * k + 8, :] = own[:, 64 * k : 64 * k + 64]
 
 
 def local(panel, solved, sketch, inverses, coupling, design, prior):
     zh, zl, x, c = (lax.axis_index(name) for name in ("zh", "zl", "x", "c"))
+
+    where = jnp.stack([x, c, zh, 32 * (c % 4), 32 * (4 * zl + x)])
 
     message = call(
         start_body,
         f32(32, 8, 128),
-        c.reshape(1),
+        where,
         panel,
         solved.T,
         sketch,
@@ -230,10 +232,11 @@
             pltpu.VMEM((32, 64), jnp.float32),
             pltpu.SemaphoreType.DMA((5,)),
         ],
+        limit=56329502,
     )
     got = exchange(message, ("x", "c"))
 
-    message = call(split_body, f32(16, 32, 128), jnp.stack([x, c]), got, specs=[SMEM, VMEM])
+    message = call(split_body, f32(16, 32, 128), where, got, specs=[SMEM, VMEM])
     got = exchange(message, ("zh", "zl"))
 
     parts = exchange(call(last_body, f32(8, 64, 128), got), "c")
@@ -242,7 +245,7 @@
         call(
             bent_body,
             f32(8, 80, 128),
-            (32 * (c % 4)).reshape(1),
+            where,
             parts,
             got,
             specs=[SMEM, VMEM, VMEM],
@@ -256,7 +259,7 @@
     message = call(
         design_body,
         f32(8, 72, 256),
-        jnp.stack([c, 32 * (4 * zl + x)]),
+        where,
         first,
         last,
         design,
@@ -267,7 +270,7 @@
     block_solution, leverage = call(
         leverage_body,
         (f32(32, 64), f32(1, 256)),
-        zh.reshape(1),
+        where,
         got,
         prior.T,
         specs=[SMEM, VMEM, VMEM],

time: 117 us -> 110 us (0.940)
  blocking collectives: 36.8 us -> 101 us
  waiting for transfers between devices: 36.7 us -> 0 us
  starting transfers between devices: 29.1 us -> 0 us
  local copies, waits for them, and re-layouts: 4.39 us -> 0.73 us
    all_to_all x2 -> x6, blocking collectives: 36.8 us -> 101 us  [exchange(): return lax.all_to_all(value, axes, 0, 0, tiled=True)]
    all_to_all x4 -> x0, waiting for transfers between devices: 36.7 us -> none  [exchange(): return lax.all_to_all(value, axes, 0, 0, tiled=True)]
    all_to_all x4 -> x0, starting transfers between devices: 29.1 us -> none  [exchange(): return lax.all_to_all(value, axes, 0, 0, tiled=True)]
    unnamed x14 -> x10, local copies, waits for them, and re-layouts: 4.39 us -> 0.64 us
  transfers between devices with their start and end apart: 4 -> 0, of which waited for: 4 -> 0; matrix products, arithmetic and copies ran while one was open for 0% -> 0% of each run, Pallas kernels for 0% -> 0%
where the time goes in v5:
time: 110 us; the launch traced here: 109 us
  blocking collectives  101 us (92%)
  Pallas kernels  7.29 us (7%)
    all_to_all x6, blocking collectives, exchange(): return lax.all_to_all(value, axes, 0, 0, tiled=True)  101 us
    pallas_call x7, Pallas kernels, call(): pl.pallas_call(body, out_shape=out, in_specs=specs or [VMEM] * len(args),...  7.29 us

profile of v5, /device:TPU:1, one launch (start us, length us, event | category | flops | bytes accessed | tf_op | source)
XLA Modules:
  0.0 109.5 jit_solution(4805114456504856929)
XLA Ops:
  0.6 0.0 copy-start.4
  0.7 0.0 copy-start.3
  0.7 0.0 copy-start.2
  0.7 0.1 stack.23.where
  0.8 0.6 copy-done.4
  1.3 0.0 copy-done.3
  1.4 0.0 copy-done.2
  1.4 2.6 %shard_map.86 = f32[32,8,128]{2,1,0:T(8,128)S(1)} custom-call(s32[5]{0:T(128)S(1)} %stack.23.where, f32[32,4096]{1,0:T(8,128)} %panel_hbm.1, f32[64,4096]{1,0:T(8,128)} %bitcast.9, f32[32,64]{1,0:T(8,128)S(1)} %copy-done.2, f32[2,16,128]{2,1,0:T(8,128)S(1)} %copy-done.3, f32[16,128]{1,0:T(8,128)S(1)} %copy-done.4), custom_call_target="tpu_custom_call" | custom-call | tf_op jit(solution)/shard_map/pallas_call | solution.py:33
  4.0 17.3 %all_to_all.30.got = f32[32,8,128]{2,1,0:T(8,128)S(1)} all-to-all(f32[32,8,128]{2,1,0:T(8,128)S(1)} %shard_map.86), channel_id=1, replica_groups=mesh['zh'=8,'zl'=2,'x'=4,'c'=8] {'x','c'}, dimensions={0} | all-to-all | bytes 262144 | tf_op jit(solution)/shard_map/all_to_all | solution.py:20
  21.3 0.8 shard_map.87
  22.1 27.5 %all_to_all.31.got = f32[16,32,128]{2,1,0:T(8,128)S(1)} all-to-all(f32[16,32,128]{2,1,0:T(8,128)S(1)} %shard_map.87), channel_id=1, replica_groups=mesh['zh'=8,'zl'=2,'x'=4,'c'=8] {'zh','zl'}, dimensions={0} | all-to-all | bytes 524288 | tf_op jit(solution)/shard_map/all_to_all | solution.py:20
  49.6 0.3 shard_map.88
  49.9 14.1 %all_to_all.32.parts = f32[8,64,128]{2,1,0:T(8,128)S(1)} all-to-all(f32[8,64,128]{2,1,0:T(8,128)S(1)} %shard_map.88), channel_id=1, replica_groups=mesh['zh'=8,'zl'=2,'x'=4,'c'=8] {'c'}, dimensions={0} | all-to-all | bytes 524288 | tf_op jit(solution)/shard_map/all_to_all | solution.py:20
  64.0 0.9 shard_map.89
  64.9 10.0 %all_to_all.33.parts.last = f32[8,80,128]{2,1,0:T(8,128)S(1)} all-to-all(f32[8,80,128]{2,1,0:T(8,128)S(1)} %shard_map.89), channel_id=1, replica_groups=mesh['zh'=8,'zl'=2,'x'=4,'c'=8] {'zl','x'}, dimensions={0} | all-to-all | bytes 655360 | tf_op jit(solution)/shard_map/all_to_all | solution.py:20
  74.9 0.0 copy-start
  74.9 0.4 shard_map.90
  75.3 18.1 %all_to_all.34.first = f32[64,16,128]{2,1,0:T(8,128)S(1)} all-to-all(f32[64,16,128]{2,1,0:T(8,128)S(1)} %shard_map.90), channel_id=1, replica_groups=mesh['zh'=8,'zl'=2,'x'=4,'c'=8] {'zl','x','c'}, dimensions={0} | all-to-all | bytes 1048576 | tf_op jit(solution)/shard_map/all_to_all | solution.py:20
  93.4 0.0 copy-done
  93.4 1.1 shard_map.91
  94.5 0.0 copy-start.1
  94.5 13.7 %all_to_all.35.got = f32[8,72,256]{2,1,0:T(8,128)S(1)} all-to-all(f32[8,72,256]{2,1,0:T(8,128)S(1)} %shard_map.91), channel_id=1, replica_groups=mesh['zh'=8,'zl'=2,'x'=4,'c'=8] {'c'}, dimensions={0} | all-to-all | bytes 1179648 | tf_op jit(solution)/shard_map/all_to_all | solution.py:20
  108.2 0.0 copy-done.1
  108.2 1.2 %shard_map.92 = (f32[32,64]{1,0:T(8,128)}, f32[1,256]{1,0:T(1,128)}) custom-call(s32[5]{0:T(128)S(1)} %stack.23.where, f32[8,72,256]{2,1,0:T(8,128)S(1)} %all_to_all.35.got, f32[64,256]{1,0:T(8,128)S(1)} %bitcast.8), custom_call_target="tpu_custom_call" | custom-call | tf_op jit(solution)/shard_map/pallas_call | solution.py:33
Async XLA Ops:
  0.6 0.7 copy-start.4
  0.7 0.7 copy-start.3
  0.7 0.7 copy-start.2
  74.9 18.5 %copy-start = (bf16[2048,256]{1,0:T(8,128)(2,1)S(1)}, bf16[2048,256]{1,0:T(8,128)(2,1)}, u32[]{:S(2)}) copy-start(bf16[2048,256]{1,0:T(8,128)(2,1)} %design.1) | copy-start | bytes 3145732
  94.5 13.7 %copy-start.1 = (f32[256,64]{0,1:T(8,128)S(1)}, f32[256,64]{0,1:T(8,128)}, u32[]{:S(2)}) copy-start(f32[256,64]{0,1:T(8,128)} %param.13) | copy-start | bytes 196612

commit v6 on v4

--- a/solution.py
+++ b/solution.py
@@ -8,7 +8,6 @@
 
 HIGHEST = lax.Precision.HIGHEST
 VMEM = pl.BlockSpec(memory_space=pltpu.VMEM)
-SMEM = pl.BlockSpec(memory_space=pltpu.SMEM)
 NT = (((1,), (1,)), ((), ()))
 
 
@@ -65,7 +64,7 @@
     return out
 
 
-def start_body(column, panel_hbm, solved_hbm, sketch_hbm, inverses_hbm, coupling_hbm, out, *held):
+def start_body(panel_hbm, solved_hbm, sketch_hbm, inverses_hbm, coupling_hbm, out, *held):
     sources = (inverses_hbm, coupling_hbm, panel_hbm, solved_hbm, sketch_hbm)
     inverses, coupling, panel, solved_t, sketch, sems = held
     copies = [
@@ -110,15 +109,15 @@
     )
     total = products[:32] + products[32:]
     total = total[:, :64] + total[:, 64:]
-    total = jnp.where(column[0] == 0, sketch[...], 0.0) - total
+    total = jnp.where(lax.axis_index("c") == 0, sketch[...], 0.0) - total
     for c2 in range(8):
         piece = packed(total[4 * c2 : 4 * c2 + 4])
         for x2 in range(4):
             out[8 * x2 + c2, 0:2] = piece
 
 
-def split_body(where, got, out):
-    x, c = where[0], where[1]
+def split_body(got, out):
+    x, c = lax.axis_index("x"), lax.axis_index("c")
     right = [unpacked(got[8 * k : 8 * k + 8, 0:2].sum(axis=0)) for k in range(4)]
     right = jnp.concatenate(
         [jnp.concatenate(right[:2], axis=0), jnp.concatenate(right[2:], axis=0)], axis=1
@@ -159,40 +158,43 @@
         out[k] = terms
 
 
-def bent_body(where, parts, got, out, held):
+def bent_body(parts, got, out, y_out):
     y_last = unpacked(parts[...].sum(axis=0))
-    held[...] = y_last
     bent = dot(got[:, 16:24].reshape(128, 128), y_last).reshape(8, 2, 8, 64)
     bent = jnp.concatenate([bent[:, 0].reshape(64, 64), bent[:, 1].reshape(64, 64)], axis=1)
-    piece = packed(held[pl.ds(pl.multiple_of(where[0], 32), 32), :])
-    for k in range(8):
-        out[k, :64] = bent
-        out[k, 64:] = piece
-
-
-def first_body(parts, got, out):
-    bent = parts[:, :64].sum(axis=0)
+    for k in range(8):
+        out[k] = bent
+    for g in range(4):
+        y_out[g] = packed(y_last[32 * g : 32 * g + 32])
+
+
+def first_body(parts, y_last, got, out):
+    bent = parts[...].sum(axis=0)
     right = unpacked(got[0:8, 0:8] - bent.reshape(8, 8, 128)).reshape(128, 64)
     terms = dot(got[:, 24:32].reshape(128, 128), right)
     for g in range(4):
         piece = packed(terms[32 * g : 32 * g + 32])
-        for k in range(16):
-            out[4 * k + g] = piece
-
-
-def design_body(where, first, last, design, out, held):
+        last = y_last[g]
+        for k in range(8):
+            out[8 * k + g] = piece
+            out[8 * k + 4 + g] = last
+
+
+def design_body(parts, design, out, held):
+    c = lax.axis_index("c")
     for h in range(2):
         for x in range(4):
             k = 4 * h + x
-            piece = first[8 * k : 8 * k + 8].sum(axis=0)
-            piece = jnp.where(where[0] < 4, piece, last[k, 64:80])
+            piece = parts[8 * k : 8 * k + 8].sum(axis=0)
+            piece = jnp.where(c < 4, piece, parts[8 * k])
             for z in range(4):
                 row = 64 * z + 16 * x + 8 * h
                 held[row : row + 8, :] = piece[
                     8 * (z % 2) : 8 * (z % 2) + 8, 64 * (z // 2) : 64 * (z // 2) + 64
                 ]
     turned = held[...].T.astype(jnp.bfloat16)
-    own = held[pl.ds(pl.multiple_of(where[1], 32), 32), :]
+    own = 32 * (4 * lax.axis_index("zl") + lax.axis_index("x"))
+    own = held[pl.ds(pl.multiple_of(own, 32), 32), :]
     own = jnp.concatenate([own[8 * k : 8 * k + 8] for k in range(4)], axis=1)
     for k in range(8):
         out[k, :64] = lax.dot_general(
@@ -201,27 +203,24 @@
         out[k, 64:] = own
 
 
-def leverage_body(where, got, prior_t, solution_rows, leverage):
+def leverage_body(got, prior_t, solution_rows, leverage):
     total = prior_t[...] + got[:, :64].sum(axis=0)
     leverage[...] = jnp.sum(total * total, axis=0, keepdims=True) * (1.0 / 64)
-    own = got[where[0], 64:72]
+    own = got[lax.axis_index("zh"), 64:72]
     for k in range(4):
         solution_rows[8 * k : 8 * k + 8, :] = own[:, 64 * k : 64 * k + 64]
 
 
 def local(panel, solved, sketch, inverses, coupling, design, prior):
-    zh, zl, x, c = (lax.axis_index(name) for name in ("zh", "zl", "x", "c"))
-
     message = call(
         start_body,
         f32(32, 8, 128),
-        c.reshape(1),
         panel,
         solved.T,
         sketch,
         inverses,
         coupling,
-        specs=[SMEM] + [pl.BlockSpec(memory_space=pl.ANY)] * 5,
+        specs=[pl.BlockSpec(memory_space=pl.ANY)] * 5,
         scratch=[
             pltpu.VMEM((2, 16, 128), jnp.float32),
             pltpu.VMEM((16, 128), jnp.float32),
@@ -230,48 +229,24 @@
             pltpu.VMEM((32, 64), jnp.float32),
             pltpu.SemaphoreType.DMA((5,)),
         ],
+        limit=60 << 20,
     )
     got = exchange(message, ("x", "c"))
 
-    message = call(split_body, f32(16, 32, 128), jnp.stack([x, c]), got, specs=[SMEM, VMEM])
-    got = exchange(message, ("zh", "zl"))
+    got = exchange(call(split_body, f32(16, 32, 128), got), ("zh", "zl"))
 
     parts = exchange(call(last_body, f32(8, 64, 128), got), "c")
 
-    last = exchange(
-        call(
-            bent_body,
-            f32(8, 80, 128),
-            (32 * (c % 4)).reshape(1),
-            parts,
-            got,
-            specs=[SMEM, VMEM, VMEM],
-            scratch=[pltpu.VMEM((128, 64), jnp.float32)],
-        ),
-        ("zl", "x"),
-    )
-
-    first = exchange(call(first_body, f32(64, 16, 128), last, got), ("zl", "x", "c"))
+    bent, y_last = call(bent_body, (f32(8, 64, 128), f32(4, 16, 128)), parts, got)
+    parts = exchange(bent, ("zl", "x"))
+
+    parts = exchange(call(first_body, f32(64, 16, 128), parts, y_last, got), ("zl", "x", "c"))
 
     message = call(
-        design_body,
-        f32(8, 72, 256),
-        jnp.stack([c, 32 * (4 * zl + x)]),
-        first,
-        last,
-        design,
-        specs=[SMEM, VMEM, VMEM, VMEM],
-        scratch=[pltpu.VMEM((256, 64), jnp.float32)],
+        design_body, f32(8, 72, 256), parts, design, scratch=[pltpu.VMEM((256, 64), jnp.float32)]
     )
     got = exchange(message, "c")
-    block_solution, leverage = call(
-        leverage_body,
-        (f32(32, 64), f32(1, 256)),
-        zh.reshape(1),
-        got,
-        prior.T,
-        specs=[SMEM, VMEM, VMEM],
-    )
+    block_solution, leverage = call(leverage_body, (f32(32, 64), f32(1, 256)), got, prior.T)
     return block_solution, leverage.reshape(256)
 
 

time: 117 us -> 107 us (0.915)
  blocking collectives: 36.8 us -> 101 us
  waiting for transfers between devices: 36.7 us -> 0 us
  starting transfers between devices: 29.1 us -> 0 us
  local copies, waits for them, and re-layouts: 4.39 us -> 0.01 us
  Pallas kernels: 8.05 us -> 5.2 us
    all_to_all x2 -> x6, blocking collectives: 36.8 us -> 101 us  [exchange(): return lax.all_to_all(value, axes, 0, 0, tiled=True)]
    all_to_all x4 -> x0, waiting for transfers between devices: 36.7 us -> none  [exchange(): return lax.all_to_all(value, axes, 0, 0, tiled=True)]
    all_to_all x4 -> x0, starting transfers between devices: 29.1 us -> none  [exchange(): return lax.all_to_all(value, axes, 0, 0, tiled=True)]
    unnamed x14 -> x4, local copies, waits for them, and re-layouts: 4.39 us -> 0.01 us
    pallas_call x7, Pallas kernels: 8.05 us -> 5.2 us  [call(): pl.pallas_call(body, out_shape=out, in_specs=specs or [VMEM] * len(args),...]
  transfers between devices with their start and end apart: 4 -> 0, of which waited for: 4 -> 0; matrix products, arithmetic and copies ran while one was open for 0% -> 0% of each run, Pallas kernels for 0% -> 0%
where the time goes in v6:
time: 107 us; the launch traced here: 106 us
  blocking collectives  101 us (94%)
  Pallas kernels  5.2 us (5%)
    all_to_all x6, blocking collectives, exchange(): return lax.all_to_all(value, axes, 0, 0, tiled=True)  101 us
    pallas_call x7, Pallas kernels, call(): pl.pallas_call(body, out_shape=out, in_specs=specs or [VMEM] * len(args),...  5.2 us

profile of v6, /device:TPU:1, one launch (start us, length us, event | category | flops | bytes accessed | tf_op | source)
XLA Modules:
  0.0 106.5 jit_solution(14742890614407798240)
XLA Ops:
  0.6 2.7 %shard_map.86 = f32[32,8,128]{2,1,0:T(8,128)} custom-call(f32[32,4096]{1,0:T(8,128)} %panel_hbm.1, f32[64,4096]{1,0:T(8,128)} %bitcast.4, f32[32,64]{1,0:T(8,128)} %sketch_hbm.1, f32[2,16,128]{2,1,0:T(8,128)} %inverses_hbm.1, f32[16,128]{1,0:T(8,128)} %coupling_hbm.1), custom_call_target="tpu_custom_call" | custom-call | tf_op jit(solution)/shard_map/pallas_call | solution.py:32
  3.4 18.2 %all_to_all.30.got = f32[32,8,128]{2,1,0:T(8,128)S(1)} all-to-all(f32[32,8,128]{2,1,0:T(8,128)} %shard_map.86), channel_id=1, replica_groups=mesh['zh'=8,'zl'=2,'x'=4,'c'=8] {'x','c'}, dimensions={0} | all-to-all | bytes 262144 | tf_op jit(solution)/shard_map/all_to_all | solution.py:19
  21.6 0.2 shard_map.87
  21.8 26.8 %all_to_all.31.got = f32[16,32,128]{2,1,0:T(8,128)S(1)} all-to-all(f32[16,32,128]{2,1,0:T(8,128)S(1)} %shard_map.87), channel_id=1, replica_groups=mesh['zh'=8,'zl'=2,'x'=4,'c'=8] {'zh','zl'}, dimensions={0} | all-to-all | bytes 524288 | tf_op jit(solution)/shard_map/all_to_all | solution.py:19
  48.6 0.3 shard_map.88
  48.9 14.1 %all_to_all.32.parts = f32[8,64,128]{2,1,0:T(8,128)S(1)} all-to-all(f32[8,64,128]{2,1,0:T(8,128)S(1)} %shard_map.88), channel_id=1, replica_groups=mesh['zh'=8,'zl'=2,'x'=4,'c'=8] {'c'}, dimensions={0} | all-to-all | bytes 524288 | tf_op jit(solution)/shard_map/all_to_all | solution.py:19
  63.0 0.3 shard_map.89
  63.4 9.4 %all_to_all.33.parts = f32[8,64,128]{2,1,0:T(8,128)S(1)} all-to-all(f32[8,64,128]{2,1,0:T(8,128)S(1)} %get-tuple-element.6), channel_id=1, replica_groups=mesh['zh'=8,'zl'=2,'x'=4,'c'=8] {'zl','x'}, dimensions={0} | all-to-all | bytes 524288 | tf_op jit(solution)/shard_map/all_to_all | solution.py:19
  72.8 0.0 copy-start
  72.8 0.3 shard_map.90
  73.1 18.4 %all_to_all.34.parts = f32[64,16,128]{2,1,0:T(8,128)S(1)} all-to-all(f32[64,16,128]{2,1,0:T(8,128)S(1)} %shard_map.90), channel_id=1, replica_groups=mesh['zh'=8,'zl'=2,'x'=4,'c'=8] {'zl','x','c'}, dimensions={0} | all-to-all | bytes 1048576 | tf_op jit(solution)/shard_map/all_to_all | solution.py:19
  91.5 0.0 copy-done
  91.5 0.5 shard_map.91
  92.0 0.0 copy-start.1
  92.0 13.7 %all_to_all.35.got = f32[8,72,256]{2,1,0:T(8,128)S(1)} all-to-all(f32[8,72,256]{2,1,0:T(8,128)S(1)} %shard_map.91), channel_id=1, replica_groups=mesh['zh'=8,'zl'=2,'x'=4,'c'=8] {'c'}, dimensions={0} | all-to-all | bytes 1179648 | tf_op jit(solution)/shard_map/all_to_all | solution.py:19
  105.8 0.0 copy-done.1
  105.8 0.7 shard_map.92
Async XLA Ops:
  72.8 18.7 %copy-start = (bf16[2048,256]{1,0:T(8,128)(2,1)S(1)}, bf16[2048,256]{1,0:T(8,128)(2,1)}, u32[]{:S(2)}) copy-start(bf16[2048,256]{1,0:T(8,128)(2,1)} %design.1) | copy-start | bytes 3145732
  92.0 13.7 %copy-start.1 = (f32[256,64]{0,1:T(8,128)S(1)}, f32[256,64]{0,1:T(8,128)}, u32[]{:S(2)}) copy-start(f32[256,64]{0,1:T(8,128)} %param.13) | copy-start | bytes 196612

commit v7 on v6

--- a/solution.py
+++ b/solution.py
@@ -9,6 +9,7 @@
 HIGHEST = lax.Precision.HIGHEST
 VMEM = pl.BlockSpec(memory_space=pltpu.VMEM)
 NT = (((1,), (1,)), ((), ()))
+CHUNKS = 4
 
 
 def dot(a, b):
@@ -65,11 +66,14 @@
 
 
 def start_body(panel_hbm, solved_hbm, sketch_hbm, inverses_hbm, coupling_hbm, out, *held):
-    sources = (inverses_hbm, coupling_hbm, panel_hbm, solved_hbm, sketch_hbm)
-    inverses, coupling, panel, solved_t, sketch, sems = held
+    inverses, coupling, sketch, panel, solved_t, sems = held
+    pairs = [(inverses_hbm, inverses), (coupling_hbm, coupling), (sketch_hbm, sketch)]
+    for k in range(CHUNKS):
+        span = pl.ds(k * (4096 // CHUNKS), 4096 // CHUNKS)
+        pairs += [(solved_hbm.at[:, span], solved_t.at[k]), (panel_hbm.at[:, span], panel.at[k])]
     copies = [
         pltpu.make_async_copy(source, target, sems.at[k])
-        for k, (source, target) in enumerate(zip(sources, held))
+        for k, (source, target) in enumerate(pairs)
     ]
     for copy in copies:
         copy.start()
@@ -102,11 +106,14 @@
             out[8 * x2 + g, 7:8] = piece
             out[8 * x2 + 4 + g, 7:8] = piece
 
-    for copy in copies[2:]:
-        copy.wait()
-    products = lax.dot_general(
-        two_parts(panel[...]), two_parts(solved_t[...]), NT, preferred_element_type=jnp.float32
-    )
+    copies[2].wait()
+    products = jnp.zeros((64, 128), jnp.float32)
+    for k in range(CHUNKS):
+        copies[3 + 2 * k].wait()
+        copies[4 + 2 * k].wait()
+        products += lax.dot_general(
+            two_parts(panel[k]), two_parts(solved_t[k]), NT, preferred_element_type=jnp.float32
+        )
     total = products[:32] + products[32:]
     total = total[:, :64] + total[:, 64:]
     total = jnp.where(lax.axis_index("c") == 0, sketch[...], 0.0) - total
@@ -143,17 +150,30 @@
                 halves[h] = jnp.where(here, piece, halves[h])
     halves = [staggered(half, -32, -16 * h) for h, half in enumerate(halves)]
 
-    for k in range(8):
-        for h in range(2):
-            out[2 * k + h, 0:8] = right
-            out[2 * k + h, 8:16] = mats[h]
-            out[2 * k + h, 16:24] = halves[h]
-            out[2 * k + h, 24:32] = mats[2 + h]
+    own = got[pl.ds(pl.multiple_of(8 * x, 8), 8), 0:2].sum(axis=0)
+    for h in range(2):
+        near = jnp.concatenate([mats[h][:, :64], mats[2 + h][:, :64]], axis=1)
+        far = jnp.concatenate([mats[h][:, 64:], mats[2 + h][:, 64:]], axis=1)
+        near = jnp.where(lax.axis_index("zh") < 4, near, right)
+        piece = own[:, 64 * h : 64 * h + 64]
+        piece = jnp.concatenate([piece[0:1], piece[1:2]], axis=1)
+        piece = jnp.concatenate([piece, piece], axis=0)
+        for k in range(8):
+            for m, tile in enumerate((near, far, halves[h])):
+                for j in range(4):
+                    out[2 * k + h, 4 * m + j] = tile[2 * j : 2 * j + 2]
+            out[2 * k + h, 12] = piece
+
+
+def applied(got, lanes, vector):
+    terms = dot(got[:, 8:16, lanes].reshape(128, 64), vector[64:])
+    near = dot(got[0:8, 0:8, lanes].reshape(64, 64), vector[:64])
+    return jnp.concatenate([terms[:64] + near, terms[64:]], axis=0)
 
 
 def last_body(got, out):
     right = unpacked(got[8:16, 0:8]).reshape(128, 64)
-    terms = packed(dot(got[:, 8:16].reshape(128, 128), right))
+    terms = packed(applied(got, slice(0, 64), right))
     for k in range(8):
         out[k] = terms
 
@@ -162,16 +182,26 @@
     y_last = unpacked(parts[...].sum(axis=0))
     bent = dot(got[:, 16:24].reshape(128, 128), y_last).reshape(8, 2, 8, 64)
     bent = jnp.concatenate([bent[:, 0].reshape(64, 64), bent[:, 1].reshape(64, 64)], axis=1)
+
+    x, h = lax.axis_index("x"), lax.axis_index("zl")
+    row = lax.broadcasted_iota(jnp.int32, (8, 128), 0)
+    half = lax.broadcasted_iota(jnp.int32, (8, 128), 1) // 64
+    here = (half == x // 2) & (row // 2 == 2 * (x % 2) + h)
+    rows = []
+    for z in range(8):
+        piece = got[z, 24:25]
+        piece = jnp.where(row % 2 == x // 2, piece, pltpu.roll(piece, 64, 1))
+        rows.append(jnp.where(here, piece, 0.0))
+    terms = jnp.concatenate(rows, axis=0) - bent
     for k in range(8):
-        out[k] = bent
+        out[k] = terms
     for g in range(4):
         y_out[g] = packed(y_last[32 * g : 32 * g + 32])
 
 
 def first_body(parts, y_last, got, out):
-    bent = parts[...].sum(axis=0)
-    right = unpacked(got[0:8, 0:8] - bent.reshape(8, 8, 128)).reshape(128, 64)
-    terms = dot(got[:, 24:32].reshape(128, 128), right)
+    right = unpacked(parts[...].sum(axis=0).reshape(8, 8, 128)).reshape(128, 64)
+    terms = applied(got, slice(64, 128), right)
     for g in range(4):
         piece = packed(terms[32 * g : 32 * g + 32])
         last = y_last[g]
@@ -215,25 +245,23 @@
     message = call(
         start_body,
         f32(32, 8, 128),
-        panel,
-        solved.T,
-        sketch,
-        inverses,
-        coupling,
+        *(
+            pltpu.with_memory_space_constraint(value, pltpu.HBM)
+            for value in (panel, solved.T, sketch, inverses, coupling)
+        ),
         specs=[pl.BlockSpec(memory_space=pl.ANY)] * 5,
         scratch=[
             pltpu.VMEM((2, 16, 128), jnp.float32),
             pltpu.VMEM((16, 128), jnp.float32),
-            pltpu.VMEM((32, 4096), jnp.float32),
-            pltpu.VMEM((64, 4096), jnp.float32),
             pltpu.VMEM((32, 64), jnp.float32),
-            pltpu.SemaphoreType.DMA((5,)),
+            pltpu.VMEM((CHUNKS, 32, 4096 // CHUNKS), jnp.float32),
+            pltpu.VMEM((CHUNKS, 64, 4096 // CHUNKS), jnp.float32),
+            pltpu.SemaphoreType.DMA((3 + 2 * CHUNKS,)),
         ],
-        limit=60 << 20,
     )
     got = exchange(message, ("x", "c"))
 
-    got = exchange(call(split_body, f32(16, 32, 128), got), ("zh", "zl"))
+    got = exchange(call(split_body, f32(16, 13, 2, 128), got), ("zh", "zl")).reshape(16, 26, 128)
 
     parts = exchange(call(last_body, f32(8, 64, 128), got), "c")
 

time: 107 us -> 105 us (0.981)
  blocking collectives: 101 us -> 98.9 us
    all_to_all x6, blocking collectives: 101 us -> 98.9 us  [exchange(): return lax.all_to_all(value, axes, 0, 0, tiled=True)]
where the time goes in v7:
time: 105 us
  blocking collectives  98.9 us (94%)
  Pallas kernels  5.11 us (5%)
    all_to_all x6, blocking collectives, exchange(): return lax.all_to_all(value, axes, 0, 0, tiled=True)  98.9 us
    pallas_call x7, Pallas kernels, call(): pl.pallas_call(body, out_shape=out, in_specs=specs or [VMEM] * len(args),...  5.11 us

profile of v7, /device:TPU:1, one launch (start us, length us, event | category | flops | bytes accessed | tf_op | source)
XLA Modules:
  0.0 104.8 jit_solution(15918759097624430012)
XLA Ops:
  0.6 2.5 %shard_map.86 = f32[32,8,128]{2,1,0:T(8,128)S(1)} custom-call(f32[32,4096]{1,0:T(8,128)} %panel_hbm.1, f32[64,4096]{1,0:T(8,128)} %bitcast.5, f32[32,64]{1,0:T(8,128)} %sketch_hbm.1, f32[2,16,128]{2,1,0:T(8,128)} %inverses_hbm.1, f32[16,128]{1,0:T(8,128)} %coupling_hbm.1), custom_call_target="tpu_custom_call" | custom-call | tf_op jit(solution)/shard_map/pallas_call | solution.py:33
  3.2 17.3 %all_to_all.30.got = f32[32,8,128]{2,1,0:T(8,128)S(1)} all-to-all(f32[32,8,128]{2,1,0:T(8,128)S(1)} %shard_map.86), channel_id=1, replica_groups=mesh['zh'=8,'zl'=2,'x'=4,'c'=8] {'x','c'}, dimensions={0} | all-to-all | bytes 262144 | tf_op jit(solution)/shard_map/all_to_all | solution.py:20
  20.5 0.3 shard_map.87
  20.8 26.6 %all_to_all.31 = f32[16,13,2,128]{3,2,1,0:T(2,128)S(1)} all-to-all(f32[16,13,2,128]{3,2,1,0:T(2,128)S(1)} %shard_map.87), channel_id=1, replica_groups=mesh['zh'=8,'zl'=2,'x'=4,'c'=8] {'zh','zl'}, dimensions={0} | all-to-all | bytes 425984 | tf_op jit(solution)/shard_map/all_to_all | solution.py:20
  47.4 0.1 copy.10.got
  47.4 0.4 shard_map.88
  47.8 13.0 %all_to_all.32.parts = f32[8,64,128]{2,1,0:T(8,128)S(1)} all-to-all(f32[8,64,128]{2,1,0:T(8,128)S(1)} %shard_map.88), channel_id=1, replica_groups=mesh['zh'=8,'zl'=2,'x'=4,'c'=8] {'c'}, dimensions={0} | all-to-all | bytes 524288 | tf_op jit(solution)/shard_map/all_to_all | solution.py:20
  60.8 0.3 shard_map.89
  61.2 9.9 %all_to_all.33.parts = f32[8,64,128]{2,1,0:T(8,128)S(1)} all-to-all(f32[8,64,128]{2,1,0:T(8,128)S(1)} %get-tuple-element.6), channel_id=1, replica_groups=mesh['zh'=8,'zl'=2,'x'=4,'c'=8] {'zl','x'}, dimensions={0} | all-to-all | bytes 524288 | tf_op jit(solution)/shard_map/all_to_all | solution.py:20
  71.1 0.0 copy-start
  71.1 0.4 shard_map.90
  71.4 18.4 %all_to_all.34.parts = f32[64,16,128]{2,1,0:T(8,128)S(1)} all-to-all(f32[64,16,128]{2,1,0:T(8,128)S(1)} %shard_map.90), channel_id=1, replica_groups=mesh['zh'=8,'zl'=2,'x'=4,'c'=8] {'zl','x','c'}, dimensions={0} | all-to-all | bytes 1048576 | tf_op jit(solution)/shard_map/all_to_all | solution.py:20
  89.8 0.0 copy-done
  89.8 0.5 shard_map.91
  90.3 0.0 copy-start.1
  90.4 13.7 %all_to_all.35.got = f32[8,72,256]{2,1,0:T(8,128)S(1)} all-to-all(f32[8,72,256]{2,1,0:T(8,128)S(1)} %shard_map.91), channel_id=1, replica_groups=mesh['zh'=8,'zl'=2,'x'=4,'c'=8] {'c'}, dimensions={0} | all-to-all | bytes 1179648 | tf_op jit(solution)/shard_map/all_to_all | solution.py:20
  104.1 0.0 copy-done.1
  104.1 0.7 shard_map.92
  (1 shorter events, 0.0 us)
Async XLA Ops:
  71.1 18.7 %copy-start = (bf16[2048,256]{1,0:T(8,128)(2,1)S(1)}, bf16[2048,256]{1,0:T(8,128)(2,1)}, u32[]{:S(2)}) copy-start(bf16[2048,256]{1,0:T(8,128)(2,1)} %design.1) | copy-start | bytes 3145732
  90.3 13.7 %copy-start.1 = (f32[256,64]{0,1:T(8,128)S(1)}, f32[256,64]{0,1:T(8,128)}, u32[]{:S(2)}) copy-start(f32[256,64]{0,1:T(8,128)} %param.13) | copy-start | bytes 196612

commit v8 on v7

--- a/solution.py
+++ b/solution.py
@@ -199,24 +199,26 @@
         y_out[g] = packed(y_last[32 * g : 32 * g + 32])
 
 
-def first_body(parts, y_last, got, out):
+def first_body(parts, got, out):
     right = unpacked(parts[...].sum(axis=0).reshape(8, 8, 128)).reshape(128, 64)
     terms = applied(got, slice(64, 128), right)
     for g in range(4):
         piece = packed(terms[32 * g : 32 * g + 32])
-        last = y_last[g]
-        for k in range(8):
-            out[8 * k + g] = piece
-            out[8 * k + 4 + g] = last
+        out[g] = piece
+        out[4 + g] = piece
+
+
+def own_body(parts, y_last, out):
+    c = lax.axis_index("c")
+    piece = jnp.where(c < 4, parts[...].sum(axis=0), y_last[c % 4])
+    for k in range(8):
+        out[k] = piece
 
 
 def design_body(parts, design, out, held):
-    c = lax.axis_index("c")
     for h in range(2):
         for x in range(4):
-            k = 4 * h + x
-            piece = parts[8 * k : 8 * k + 8].sum(axis=0)
-            piece = jnp.where(c < 4, piece, parts[8 * k])
+            piece = parts[4 * h + x]
             for z in range(4):
                 row = 64 * z + 16 * x + 8 * h
                 held[row : row + 8, :] = piece[
@@ -268,7 +270,8 @@
     bent, y_last = call(bent_body, (f32(8, 64, 128), f32(4, 16, 128)), parts, got)
     parts = exchange(bent, ("zl", "x"))
 
-    parts = exchange(call(first_body, f32(64, 16, 128), parts, y_last, got), ("zl", "x", "c"))
+    parts = exchange(call(first_body, f32(8, 16, 128), parts, got), "c")
+    parts = exchange(call(own_body, f32(8, 16, 128), parts, y_last), ("zl", "x"))
 
     message = call(
         design_body, f32(8, 72, 256), parts, design, scratch=[pltpu.VMEM((256, 64), jnp.float32)]

time: 105 us -> 105 us (level)
    all_to_all x6 -> x7, blocking collectives: 98.9 us -> 99 us  [exchange(): return lax.all_to_all(value, axes, 0, 0, tiled=True)]
    pallas_call x7 -> x8, Pallas kernels: 5.11 us -> 5.09 us  [call(): pl.pallas_call(body, out_shape=out, in_specs=specs or [VMEM] * len(args),...]
where the time goes in v8:
time: 105 us
  blocking collectives  99 us (94%)
  Pallas kernels  5.09 us (5%)
    all_to_all x7, blocking collectives, exchange(): return lax.all_to_all(value, axes, 0, 0, tiled=True)  99 us
    pallas_call x8, Pallas kernels, call(): pl.pallas_call(body, out_shape=out, in_specs=specs or [VMEM] * len(args),...  5.09 us

profile of v8, /device:TPU:1, one launch (start us, length us, event | category | flops | bytes accessed | tf_op | source)
XLA Modules:
  0.0 104.9 jit_solution(17629633047211751405)
XLA Ops:
  0.6 2.5 %shard_map.86 = f32[32,8,128]{2,1,0:T(8,128)S(1)} custom-call(f32[32,4096]{1,0:T(8,128)} %panel_hbm.1, f32[64,4096]{1,0:T(8,128)} %bitcast.5, f32[32,64]{1,0:T(8,128)} %sketch_hbm.1, f32[2,16,128]{2,1,0:T(8,128)} %inverses_hbm.1, f32[16,128]{1,0:T(8,128)} %coupling_hbm.1), custom_call_target="tpu_custom_call" | custom-call | tf_op jit(solution)/shard_map/pallas_call | solution.py:33
  3.2 17.3 %all_to_all.35.got = f32[32,8,128]{2,1,0:T(8,128)S(1)} all-to-all(f32[32,8,128]{2,1,0:T(8,128)S(1)} %shard_map.86), channel_id=1, replica_groups=mesh['zh'=8,'zl'=2,'x'=4,'c'=8] {'x','c'}, dimensions={0} | all-to-all | bytes 262144 | tf_op jit(solution)/shard_map/all_to_all | solution.py:20
  20.5 0.3 shard_map.87
  20.8 26.6 %all_to_all.36 = f32[16,13,2,128]{3,2,1,0:T(2,128)S(1)} all-to-all(f32[16,13,2,128]{3,2,1,0:T(2,128)S(1)} %shard_map.87), channel_id=1, replica_groups=mesh['zh'=8,'zl'=2,'x'=4,'c'=8] {'zh','zl'}, dimensions={0} | all-to-all | bytes 425984 | tf_op jit(solution)/shard_map/all_to_all | solution.py:20
  47.4 0.1 copy.10.got
  47.4 0.4 shard_map.88
  47.8 13.0 %all_to_all.37.parts = f32[8,64,128]{2,1,0:T(8,128)S(1)} all-to-all(f32[8,64,128]{2,1,0:T(8,128)S(1)} %shard_map.88), channel_id=1, replica_groups=mesh['zh'=8,'zl'=2,'x'=4,'c'=8] {'c'}, dimensions={0} | all-to-all | bytes 524288 | tf_op jit(solution)/shard_map/all_to_all | solution.py:20
  60.8 0.0 copy-start
  60.8 0.3 shard_map.89
  61.2 9.9 %all_to_all.38.parts = f32[8,64,128]{2,1,0:T(8,128)S(1)} all-to-all(f32[8,64,128]{2,1,0:T(8,128)S(1)} %get-tuple-element.6), channel_id=1, replica_groups=mesh['zh'=8,'zl'=2,'x'=4,'c'=8] {'zl','x'}, dimensions={0} | all-to-all | bytes 524288 | tf_op jit(solution)/shard_map/all_to_all | solution.py:20
  71.1 0.4 shard_map.90
  71.4 9.6 %all_to_all.39.parts = f32[8,16,128]{2,1,0:T(8,128)S(1)} all-to-all(f32[8,16,128]{2,1,0:T(8,128)S(1)} %shard_map.90), channel_id=1, replica_groups=mesh['zh'=8,'zl'=2,'x'=4,'c'=8] {'c'}, dimensions={0} | all-to-all | bytes 131072 | tf_op jit(solution)/shard_map/all_to_all | solution.py:20
  81.1 7.6 %all_to_all.40.parts = f32[8,16,128]{2,1,0:T(8,128)S(1)} all-to-all(f32[8,16,128]{2,1,0:T(8,128)S(1)} %shard_map.91), channel_id=1, replica_groups=mesh['zh'=8,'zl'=2,'x'=4,'c'=8] {'zl','x'}, dimensions={0} | all-to-all | bytes 131072 | tf_op jit(solution)/shard_map/all_to_all | solution.py:20
  88.7 0.0 copy-done
  88.7 0.5 shard_map.92
  89.2 0.0 copy-start.1
  89.2 15.0 %all_to_all.41.got = f32[8,72,256]{2,1,0:T(8,128)S(1)} all-to-all(f32[8,72,256]{2,1,0:T(8,128)S(1)} %shard_map.92), channel_id=1, replica_groups=mesh['zh'=8,'zl'=2,'x'=4,'c'=8] {'c'}, dimensions={0} | all-to-all | bytes 1179648 | tf_op jit(solution)/shard_map/all_to_all | solution.py:20
  104.2 0.0 copy-done.1
  104.2 0.7 shard_map.93
  (2 shorter events, 0.0 us)
Async XLA Ops:
  60.8 27.9 %copy-start = (bf16[2048,256]{1,0:T(8,128)(2,1)S(1)}, bf16[2048,256]{1,0:T(8,128)(2,1)}, u32[]{:S(2)}) copy-start(bf16[2048,256]{1,0:T(8,128)(2,1)} %design.1) | copy-start | bytes 3145732
  89.2 15.0 %copy-start.1 = (f32[256,64]{0,1:T(8,128)S(1)}, f32[256,64]{0,1:T(8,128)}, u32[]{:S(2)}) copy-start(f32[256,64]{0,1:T(8,128)} %param.13) | copy-start | bytes 196612

commit v9 on v7

--- a/solution.py
+++ b/solution.py
@@ -9,7 +9,7 @@
 HIGHEST = lax.Precision.HIGHEST
 VMEM = pl.BlockSpec(memory_space=pltpu.VMEM)
 NT = (((1,), (1,)), ((), ()))
-CHUNKS = 4
+CHUNKS = 1
 
 
 def dot(a, b):

time: 105 us -> 105 us (level)
  no operation moved by 1% of the time
where the time goes in v9:
time: 105 us; the launch traced here: 104 us
  blocking collectives  98.9 us (94%)
  Pallas kernels  4.64 us (4%)
    all_to_all x6, blocking collectives, exchange(): return lax.all_to_all(value, axes, 0, 0, tiled=True)  98.9 us
    pallas_call x7, Pallas kernels, call(): pl.pallas_call(body, out_shape=out, in_specs=specs or [VMEM] * len(args),...  4.64 us

profile of v9, /device:TPU:1, one launch (start us, length us, event | category | flops | bytes accessed | tf_op | source)
XLA Modules:
  0.0 104.3 jit_solution(5285189178235496656)
XLA Ops:
  0.6 2.1 %shard_map.86 = f32[32,8,128]{2,1,0:T(8,128)S(1)} custom-call(f32[32,4096]{1,0:T(8,128)} %panel_hbm.1, f32[64,4096]{1,0:T(8,128)} %bitcast.5, f32[32,64]{1,0:T(8,128)} %sketch_hbm.1, f32[2,16,128]{2,1,0:T(8,128)} %inverses_hbm.1, f32[16,128]{1,0:T(8,128)} %coupling_hbm.1), custom_call_target="tpu_custom_call" | custom-call | tf_op jit(solution)/shard_map/pallas_call | solution.py:33
  2.7 17.3 %all_to_all.30.got = f32[32,8,128]{2,1,0:T(8,128)S(1)} all-to-all(f32[32,8,128]{2,1,0:T(8,128)S(1)} %shard_map.86), channel_id=1, replica_groups=mesh['zh'=8,'zl'=2,'x'=4,'c'=8] {'x','c'}, dimensions={0} | all-to-all | bytes 262144 | tf_op jit(solution)/shard_map/all_to_all | solution.py:20
  20.0 0.3 shard_map.87
  20.3 26.6 %all_to_all.31 = f32[16,13,2,128]{3,2,1,0:T(2,128)S(1)} all-to-all(f32[16,13,2,128]{3,2,1,0:T(2,128)S(1)} %shard_map.87), channel_id=1, replica_groups=mesh['zh'=8,'zl'=2,'x'=4,'c'=8] {'zh','zl'}, dimensions={0} | all-to-all | bytes 425984 | tf_op jit(solution)/shard_map/all_to_all | solution.py:20
  46.9 0.1 copy.10.got
  47.0 0.4 shard_map.88
  47.3 13.0 %all_to_all.32.parts = f32[8,64,128]{2,1,0:T(8,128)S(1)} all-to-all(f32[8,64,128]{2,1,0:T(8,128)S(1)} %shard_map.88), channel_id=1, replica_groups=mesh['zh'=8,'zl'=2,'x'=4,'c'=8] {'c'}, dimensions={0} | all-to-all | bytes 524288 | tf_op jit(solution)/shard_map/all_to_all | solution.py:20
  60.4 0.3 shard_map.89
  60.7 9.9 %all_to_all.33.parts = f32[8,64,128]{2,1,0:T(8,128)S(1)} all-to-all(f32[8,64,128]{2,1,0:T(8,128)S(1)} %get-tuple-element.6), channel_id=1, replica_groups=mesh['zh'=8,'zl'=2,'x'=4,'c'=8] {'zl','x'}, dimensions={0} | all-to-all | bytes 524288 | tf_op jit(solution)/shard_map/all_to_all | solution.py:20
  70.6 0.0 copy-start
  70.6 0.4 shard_map.90
  71.0 18.4 %all_to_all.34.parts = f32[64,16,128]{2,1,0:T(8,128)S(1)} all-to-all(f32[64,16,128]{2,1,0:T(8,128)S(1)} %shard_map.90), channel_id=1, replica_groups=mesh['zh'=8,'zl'=2,'x'=4,'c'=8] {'zl','x','c'}, dimensions={0} | all-to-all | bytes 1048576 | tf_op jit(solution)/shard_map/all_to_all | solution.py:20
  89.3 0.0 copy-done
  89.3 0.5 shard_map.91
  89.9 0.0 copy-start.1
  89.9 13.7 %all_to_all.35.got = f32[8,72,256]{2,1,0:T(8,128)S(1)} all-to-all(f32[8,72,256]{2,1,0:T(8,128)S(1)} %shard_map.91), channel_id=1, replica_groups=mesh['zh'=8,'zl'=2,'x'=4,'c'=8] {'c'}, dimensions={0} | all-to-all | bytes 1179648 | tf_op jit(solution)/shard_map/all_to_all | solution.py:20
  103.6 0.0 copy-done.1
  103.6 0.7 shard_map.92
  (1 shorter events, 0.0 us)
Async XLA Ops:
  70.6 18.7 %copy-start = (bf16[2048,256]{1,0:T(8,128)(2,1)S(1)}, bf16[2048,256]{1,0:T(8,128)(2,1)}, u32[]{:S(2)}) copy-start(bf16[2048,256]{1,0:T(8,128)(2,1)} %design.1) | copy-start | bytes 3145732
  89.9 13.7 %copy-start.1 = (f32[256,64]{0,1:T(8,128)S(1)}, f32[256,64]{0,1:T(8,128)}, u32[]{:S(2)}) copy-start(f32[256,64]{0,1:T(8,128)} %param.13) | copy-start | bytes 196612

commit v10 on v8

--- a/solution.py
+++ b/solution.py
@@ -9,7 +9,7 @@
 HIGHEST = lax.Precision.HIGHEST
 VMEM = pl.BlockSpec(memory_space=pltpu.VMEM)
 NT = (((1,), (1,)), ((), ()))
-CHUNKS = 4
+CHUNKS = 1
 
 
 def dot(a, b):
@@ -202,45 +202,52 @@
 def first_body(parts, got, out):
     right = unpacked(parts[...].sum(axis=0).reshape(8, 8, 128)).reshape(128, 64)
     terms = applied(got, slice(64, 128), right)
-    for g in range(4):
-        piece = packed(terms[32 * g : 32 * g + 32])
-        out[g] = piece
-        out[4 + g] = piece
+    pieces = [packed(terms[32 * g : 32 * g + 32]) for g in range(4)]
+    block = lax.axis_index("zh") % 4
+    shown = pieces[0]
+    for g in range(1, 4):
+        shown = jnp.where(block == g, pieces[g], shown)
+    for k in range(8):
+        out[k, 0:16] = pieces[k % 4]
+        out[k, 16:32] = shown
 
 
 def own_body(parts, y_last, out):
-    c = lax.axis_index("c")
-    piece = jnp.where(c < 4, parts[...].sum(axis=0), y_last[c % 4])
-    for k in range(8):
-        out[k] = piece
-
-
-def design_body(parts, design, out, held):
+    c, zh = lax.axis_index("c"), lax.axis_index("zh")
+    total = parts[...].sum(axis=0)
+    piece = jnp.where(c < 4, total[:16], y_last[c % 4])
+    shown = jnp.where(zh < 4, total[16:], y_last[zh % 4])
+    for k in range(8):
+        out[k, 0:16] = piece
+        half = k % 4 // 2
+        out[k, 16:24] = shown[8 * half : 8 * half + 8]
+
+
+def design_body(parts, design, out, solution_rows, held):
     for h in range(2):
         for x in range(4):
-            piece = parts[4 * h + x]
+            piece = parts[4 * h + x, 0:16]
             for z in range(4):
                 row = 64 * z + 16 * x + 8 * h
                 held[row : row + 8, :] = piece[
                     8 * (z % 2) : 8 * (z % 2) + 8, 64 * (z // 2) : 64 * (z // 2) + 64
                 ]
     turned = held[...].T.astype(jnp.bfloat16)
-    own = 32 * (4 * lax.axis_index("zl") + lax.axis_index("x"))
-    own = held[pl.ds(pl.multiple_of(own, 32), 32), :]
-    own = jnp.concatenate([own[8 * k : 8 * k + 8] for k in range(4)], axis=1)
-    for k in range(8):
-        out[k, :64] = lax.dot_general(
+    for k in range(8):
+        out[k] = lax.dot_general(
             turned, design[256 * k : 256 * k + 256], NT, preferred_element_type=jnp.float32
         )
-        out[k, 64:] = own
-
-
-def leverage_body(got, prior_t, solution_rows, leverage):
-    total = prior_t[...] + got[:, :64].sum(axis=0)
+    x, zl = lax.axis_index("x"), lax.axis_index("zl")
+    for b in range(2):
+        for h in range(2):
+            piece = parts[4 * h + 2 * (x % 2) + b, 16:24]
+            row = 16 * b + 8 * h
+            solution_rows[row : row + 8, :] = jnp.where(zl == 0, piece[:, :64], piece[:, 64:])
+
+
+def leverage_body(got, prior_t, leverage):
+    total = prior_t[...] + got[...].sum(axis=0)
     leverage[...] = jnp.sum(total * total, axis=0, keepdims=True) * (1.0 / 64)
-    own = got[lax.axis_index("zh"), 64:72]
-    for k in range(4):
-        solution_rows[8 * k : 8 * k + 8, :] = own[:, 64 * k : 64 * k + 64]
 
 
 def local(panel, solved, sketch, inverses, coupling, design, prior):
@@ -270,14 +277,17 @@
     bent, y_last = call(bent_body, (f32(8, 64, 128), f32(4, 16, 128)), parts, got)
     parts = exchange(bent, ("zl", "x"))
 
-    parts = exchange(call(first_body, f32(8, 16, 128), parts, got), "c")
-    parts = exchange(call(own_body, f32(8, 16, 128), parts, y_last), ("zl", "x"))
-
-    message = call(
-        design_body, f32(8, 72, 256), parts, design, scratch=[pltpu.VMEM((256, 64), jnp.float32)]
-    )
-    got = exchange(message, "c")
-    block_solution, leverage = call(leverage_body, (f32(32, 64), f32(1, 256)), got, prior.T)
+    parts = exchange(call(first_body, f32(8, 32, 128), parts, got), "c")
+    parts = exchange(call(own_body, f32(8, 24, 128), parts, y_last), ("zl", "x"))
+
+    message, block_solution = call(
+        design_body,
+        (f32(8, 64, 256), f32(32, 64)),
+        parts,
+        design,
+        scratch=[pltpu.VMEM((256, 64), jnp.float32)],
+    )
+    leverage = call(leverage_body, f32(1, 256), exchange(message, "c"), prior.T)
     return block_solution, leverage.reshape(256)
 
 

time: 105 us -> 105 us (level)
  no operation moved by 1% of the time
where the time goes in v10:
time: 105 us
  blocking collectives  98.8 us (94%)
  Pallas kernels  5.09 us (5%)
    all_to_all x7, blocking collectives, exchange(): return lax.all_to_all(value, axes, 0, 0, tiled=True)  98.8 us
    pallas_call x8, Pallas kernels, call(): pl.pallas_call(body, out_shape=out, in_specs=specs or [VMEM] * len(args),...  5.09 us

profile of v10, /device:TPU:1, one launch (start us, length us, event | category | flops | bytes accessed | tf_op | source)
XLA Modules:
  0.0 104.7 jit_solution(12478297555164038708)
XLA Ops:
  0.6 2.1 %shard_map.86 = f32[32,8,128]{2,1,0:T(8,128)S(1)} custom-call(f32[32,4096]{1,0:T(8,128)} %panel_hbm.1, f32[64,4096]{1,0:T(8,128)} %bitcast.5, f32[32,64]{1,0:T(8,128)} %sketch_hbm.1, f32[2,16,128]{2,1,0:T(8,128)} %inverses_hbm.1, f32[16,128]{1,0:T(8,128)} %coupling_hbm.1), custom_call_target="tpu_custom_call" | custom-call | tf_op jit(solution)/shard_map/pallas_call | solution.py:33
  2.7 17.3 %all_to_all.35.got = f32[32,8,128]{2,1,0:T(8,128)S(1)} all-to-all(f32[32,8,128]{2,1,0:T(8,128)S(1)} %shard_map.86), channel_id=1, replica_groups=mesh['zh'=8,'zl'=2,'x'=4,'c'=8] {'x','c'}, dimensions={0} | all-to-all | bytes 262144 | tf_op jit(solution)/shard_map/all_to_all | solution.py:20
  20.0 0.3 shard_map.87
  20.3 26.6 %all_to_all.36 = f32[16,13,2,128]{3,2,1,0:T(2,128)S(1)} all-to-all(f32[16,13,2,128]{3,2,1,0:T(2,128)S(1)} %shard_map.87), channel_id=1, replica_groups=mesh['zh'=8,'zl'=2,'x'=4,'c'=8] {'zh','zl'}, dimensions={0} | all-to-all | bytes 425984 | tf_op jit(solution)/shard_map/all_to_all | solution.py:20
  46.9 0.1 copy.10.got
  47.0 0.4 shard_map.88
  47.3 13.0 %all_to_all.37.parts = f32[8,64,128]{2,1,0:T(8,128)S(1)} all-to-all(f32[8,64,128]{2,1,0:T(8,128)S(1)} %shard_map.88), channel_id=1, replica_groups=mesh['zh'=8,'zl'=2,'x'=4,'c'=8] {'c'}, dimensions={0} | all-to-all | bytes 524288 | tf_op jit(solution)/shard_map/all_to_all | solution.py:20
  60.4 0.3 shard_map.89
  60.7 0.0 copy-start
  60.7 10.0 %all_to_all.38.parts = f32[8,64,128]{2,1,0:T(8,128)S(1)} all-to-all(f32[8,64,128]{2,1,0:T(8,128)S(1)} %get-tuple-element.6), channel_id=1, replica_groups=mesh['zh'=8,'zl'=2,'x'=4,'c'=8] {'zl','x'}, dimensions={0} | all-to-all | bytes 524288 | tf_op jit(solution)/shard_map/all_to_all | solution.py:20
  70.7 0.4 shard_map.90
  71.1 10.1 %all_to_all.39.parts = f32[8,32,128]{2,1,0:T(8,128)S(1)} all-to-all(f32[8,32,128]{2,1,0:T(8,128)S(1)} %shard_map.90), channel_id=1, replica_groups=mesh['zh'=8,'zl'=2,'x'=4,'c'=8] {'c'}, dimensions={0} | all-to-all | bytes 262144 | tf_op jit(solution)/shard_map/all_to_all | solution.py:20
  81.2 7.7 %all_to_all.40.parts = f32[8,24,128]{2,1,0:T(8,128)S(1)} all-to-all(f32[8,24,128]{2,1,0:T(8,128)S(1)} %shard_map.91), channel_id=1, replica_groups=mesh['zh'=8,'zl'=2,'x'=4,'c'=8] {'zl','x'}, dimensions={0} | all-to-all | bytes 196608 | tf_op jit(solution)/shard_map/all_to_all | solution.py:20
  88.9 0.0 copy-done
  88.9 1.0 shard_map.92
  89.9 0.0 copy-start.1
  89.9 14.1 %all_to_all.41.got = f32[8,64,256]{2,1,0:T(8,128)S(1)} all-to-all(f32[8,64,256]{2,1,0:T(8,128)S(1)} %get-tuple-element.9), channel_id=1, replica_groups=mesh['zh'=8,'zl'=2,'x'=4,'c'=8] {'c'}, dimensions={0} | all-to-all | bytes 1048576 | tf_op jit(solution)/shard_map/all_to_all | solution.py:20
  104.0 0.0 copy-done.1
  104.0 0.6 shard_map.93
  (2 shorter events, 0.0 us)
Async XLA Ops:
  60.7 28.2 %copy-start = (bf16[2048,256]{1,0:T(8,128)(2,1)S(1)}, bf16[2048,256]{1,0:T(8,128)(2,1)}, u32[]{:S(2)}) copy-start(bf16[2048,256]{1,0:T(8,128)(2,1)} %design.1) | copy-start | bytes 3145732
  89.9 14.1 %copy-start.1 = (f32[256,64]{0,1:T(8,128)S(1)}, f32[256,64]{0,1:T(8,128)}, u32[]{:S(2)}) copy-start(f32[256,64]{0,1:T(8,128)} %param.13) | copy-start | bytes 196612

commit v11 on v10

--- a/solution.py
+++ b/solution.py
@@ -223,7 +223,7 @@
         out[k, 16:24] = shown[8 * half : 8 * half + 8]
 
 
-def design_body(parts, design, out, solution_rows, held):
+def design_body(parts, design, out, held):
     for h in range(2):
         for x in range(4):
             piece = parts[4 * h + x, 0:16]
@@ -237,15 +237,15 @@
         out[k] = lax.dot_general(
             turned, design[256 * k : 256 * k + 256], NT, preferred_element_type=jnp.float32
         )
+
+
+def leverage_body(got, parts, prior_t, solution_rows, leverage):
     x, zl = lax.axis_index("x"), lax.axis_index("zl")
     for b in range(2):
         for h in range(2):
             piece = parts[4 * h + 2 * (x % 2) + b, 16:24]
             row = 16 * b + 8 * h
             solution_rows[row : row + 8, :] = jnp.where(zl == 0, piece[:, :64], piece[:, 64:])
-
-
-def leverage_body(got, prior_t, leverage):
     total = prior_t[...] + got[...].sum(axis=0)
     leverage[...] = jnp.sum(total * total, axis=0, keepdims=True) * (1.0 / 64)
 
@@ -280,14 +280,12 @@
     parts = exchange(call(first_body, f32(8, 32, 128), parts, got), "c")
     parts = exchange(call(own_body, f32(8, 24, 128), parts, y_last), ("zl", "x"))
 
-    message, block_solution = call(
-        design_body,
-        (f32(8, 64, 256), f32(32, 64)),
-        parts,
-        design,
-        scratch=[pltpu.VMEM((256, 64), jnp.float32)],
-    )
-    leverage = call(leverage_body, f32(1, 256), exchange(message, "c"), prior.T)
+    message = call(
+        design_body, f32(8, 64, 256), parts, design, scratch=[pltpu.VMEM((256, 64), jnp.float32)]
+    )
+    block_solution, leverage = call(
+        leverage_body, (f32(32, 64), f32(1, 256)), exchange(message, "c"), parts, prior.T
+    )
     return block_solution, leverage.reshape(256)
 
 

time: 105 us -> 105 us (level)
  no operation moved by 1% of the time
where the time goes in v11:
time: 105 us; the launch traced here: 104 us
  blocking collectives  98.8 us (94%)
  Pallas kernels  4.65 us (4%)
    all_to_all x7, blocking collectives, exchange(): return lax.all_to_all(value, axes, 0, 0, tiled=True)  98.8 us
    pallas_call x8, Pallas kernels, call(): pl.pallas_call(body, out_shape=out, in_specs=specs or [VMEM] * len(args),...  4.65 us

profile of v11, /device:TPU:1, one launch (start us, length us, event | category | flops | bytes accessed | tf_op | source)
XLA Modules:
  0.0 104.3 jit_solution(2469175521880990715)
XLA Ops:
  0.6 2.1 %shard_map.86 = f32[32,8,128]{2,1,0:T(8,128)S(1)} custom-call(f32[32,4096]{1,0:T(8,128)} %panel_hbm.1, f32[64,4096]{1,0:T(8,128)} %bitcast.5, f32[32,64]{1,0:T(8,128)} %sketch_hbm.1, f32[2,16,128]{2,1,0:T(8,128)} %inverses_hbm.1, f32[16,128]{1,0:T(8,128)} %coupling_hbm.1), custom_call_target="tpu_custom_call" | custom-call | tf_op jit(solution)/shard_map/pallas_call | solution.py:33
  2.7 17.3 %all_to_all.35.got = f32[32,8,128]{2,1,0:T(8,128)S(1)} all-to-all(f32[32,8,128]{2,1,0:T(8,128)S(1)} %shard_map.86), channel_id=1, replica_groups=mesh['zh'=8,'zl'=2,'x'=4,'c'=8] {'x','c'}, dimensions={0} | all-to-all | bytes 262144 | tf_op jit(solution)/shard_map/all_to_all | solution.py:20
  20.0 0.3 shard_map.87
  20.3 26.6 %all_to_all.36 = f32[16,13,2,128]{3,2,1,0:T(2,128)S(1)} all-to-all(f32[16,13,2,128]{3,2,1,0:T(2,128)S(1)} %shard_map.87), channel_id=1, replica_groups=mesh['zh'=8,'zl'=2,'x'=4,'c'=8] {'zh','zl'}, dimensions={0} | all-to-all | bytes 425984 | tf_op jit(solution)/shard_map/all_to_all | solution.py:20
  46.9 0.1 copy.10.got
  47.0 0.4 shard_map.88
  47.3 13.0 %all_to_all.37.parts = f32[8,64,128]{2,1,0:T(8,128)S(1)} all-to-all(f32[8,64,128]{2,1,0:T(8,128)S(1)} %shard_map.88), channel_id=1, replica_groups=mesh['zh'=8,'zl'=2,'x'=4,'c'=8] {'c'}, dimensions={0} | all-to-all | bytes 524288 | tf_op jit(solution)/shard_map/all_to_all | solution.py:20
  60.4 0.3 shard_map.89
  60.7 0.0 copy-start
  60.7 10.0 %all_to_all.38.parts = f32[8,64,128]{2,1,0:T(8,128)S(1)} all-to-all(f32[8,64,128]{2,1,0:T(8,128)S(1)} %get-tuple-element.6), channel_id=1, replica_groups=mesh['zh'=8,'zl'=2,'x'=4,'c'=8] {'zl','x'}, dimensions={0} | all-to-all | bytes 524288 | tf_op jit(solution)/shard_map/all_to_all | solution.py:20
  70.7 0.4 shard_map.90
  71.1 10.1 %all_to_all.39.parts = f32[8,32,128]{2,1,0:T(8,128)S(1)} all-to-all(f32[8,32,128]{2,1,0:T(8,128)S(1)} %shard_map.90), channel_id=1, replica_groups=mesh['zh'=8,'zl'=2,'x'=4,'c'=8] {'c'}, dimensions={0} | all-to-all | bytes 262144 | tf_op jit(solution)/shard_map/all_to_all | solution.py:20
  81.2 7.7 %all_to_all.40.parts = f32[8,24,128]{2,1,0:T(8,128)S(1)} all-to-all(f32[8,24,128]{2,1,0:T(8,128)S(1)} %shard_map.91), channel_id=1, replica_groups=mesh['zh'=8,'zl'=2,'x'=4,'c'=8] {'zl','x'}, dimensions={0} | all-to-all | bytes 196608 | tf_op jit(solution)/shard_map/all_to_all | solution.py:20
  88.9 0.0 copy-done
  88.9 0.5 shard_map.92
  89.4 0.0 copy-start.1
  89.4 14.1 %all_to_all.41.got = f32[8,64,256]{2,1,0:T(8,128)S(1)} all-to-all(f32[8,64,256]{2,1,0:T(8,128)S(1)} %shard_map.92), channel_id=1, replica_groups=mesh['zh'=8,'zl'=2,'x'=4,'c'=8] {'c'}, dimensions={0} | all-to-all | bytes 1048576 | tf_op jit(solution)/shard_map/all_to_all | solution.py:20
  103.6 0.0 copy-done.1
  103.6 0.7 shard_map.93
  (2 shorter events, 0.0 us)
Async XLA Ops:
  60.7 28.2 %copy-start = (bf16[2048,256]{1,0:T(8,128)(2,1)S(1)}, bf16[2048,256]{1,0:T(8,128)(2,1)}, u32[]{:S(2)}) copy-start(bf16[2048,256]{1,0:T(8,128)(2,1)} %design.1) | copy-start | bytes 3145732
  89.4 14.1 %copy-start.1 = (f32[256,64]{0,1:T(8,128)S(1)}, f32[256,64]{0,1:T(8,128)}, u32[]{:S(2)}) copy-start(f32[256,64]{0,1:T(8,128)} %param.13) | copy-start | bytes 196612

commit v12 on v11

--- a/solution.py
+++ b/solution.py
@@ -219,14 +219,14 @@
     shown = jnp.where(zh < 4, total[16:], y_last[zh % 4])
     for k in range(8):
         out[k, 0:16] = piece
-        half = k % 4 // 2
+        half = k // 4
         out[k, 16:24] = shown[8 * half : 8 * half + 8]
 
 
 def design_body(parts, design, out, held):
     for h in range(2):
         for x in range(4):
-            piece = parts[4 * h + x, 0:16]
+            piece = parts[2 * x + h, 0:16]
             for z in range(4):
                 row = 64 * z + 16 * x + 8 * h
                 held[row : row + 8, :] = piece[
@@ -243,7 +243,7 @@
     x, zl = lax.axis_index("x"), lax.axis_index("zl")
     for b in range(2):
         for h in range(2):
-            piece = parts[4 * h + 2 * (x % 2) + b, 16:24]
+            piece = parts[4 * (x % 2) + 2 * b + h, 16:24]
             row = 16 * b + 8 * h
             solution_rows[row : row + 8, :] = jnp.where(zl == 0, piece[:, :64], piece[:, 64:])
     total = prior_t[...] + got[...].sum(axis=0)
@@ -275,10 +275,10 @@
     parts = exchange(call(last_body, f32(8, 64, 128), got), "c")
 
     bent, y_last = call(bent_body, (f32(8, 64, 128), f32(4, 16, 128)), parts, got)
-    parts = exchange(bent, ("zl", "x"))
+    parts = exchange(bent, ("x", "zl"))
 
     parts = exchange(call(first_body, f32(8, 32, 128), parts, got), "c")
-    parts = exchange(call(own_body, f32(8, 24, 128), parts, y_last), ("zl", "x"))
+    parts = exchange(call(own_body, f32(8, 24, 128), parts, y_last), ("x", "zl"))
 
     message = call(
         design_body, f32(8, 64, 256), parts, design, scratch=[pltpu.VMEM((256, 64), jnp.float32)]

time: 105 us -> 105 us (level)
  no operation moved by 1% of the time
where the time goes in v12:
time: 105 us; the launch traced here: 104 us
  blocking collectives  98.9 us (94%)
  Pallas kernels  4.65 us (4%)
    all_to_all x7, blocking collectives, exchange(): return lax.all_to_all(value, axes, 0, 0, tiled=True)  98.9 us
    pallas_call x8, Pallas kernels, call(): pl.pallas_call(body, out_shape=out, in_specs=specs or [VMEM] * len(args),...  4.65 us

profile of v12, /device:TPU:1, one launch (start us, length us, event | category | flops | bytes accessed | tf_op | source)
XLA Modules:
  0.0 104.4 jit_solution(15451133505081375090)
XLA Ops:
  0.6 2.1 %shard_map.86 = f32[32,8,128]{2,1,0:T(8,128)S(1)} custom-call(f32[32,4096]{1,0:T(8,128)} %panel_hbm.1, f32[64,4096]{1,0:T(8,128)} %bitcast.5, f32[32,64]{1,0:T(8,128)} %sketch_hbm.1, f32[2,16,128]{2,1,0:T(8,128)} %inverses_hbm.1, f32[16,128]{1,0:T(8,128)} %coupling_hbm.1), custom_call_target="tpu_custom_call" | custom-call | tf_op jit(solution)/shard_map/pallas_call | solution.py:33
  2.7 17.3 %all_to_all.35.got = f32[32,8,128]{2,1,0:T(8,128)S(1)} all-to-all(f32[32,8,128]{2,1,0:T(8,128)S(1)} %shard_map.86), channel_id=1, replica_groups=mesh['zh'=8,'zl'=2,'x'=4,'c'=8] {'x','c'}, dimensions={0} | all-to-all | bytes 262144 | tf_op jit(solution)/shard_map/all_to_all | solution.py:20
  20.0 0.3 shard_map.87
  20.3 26.6 %all_to_all.36 = f32[16,13,2,128]{3,2,1,0:T(2,128)S(1)} all-to-all(f32[16,13,2,128]{3,2,1,0:T(2,128)S(1)} %shard_map.87), channel_id=1, replica_groups=mesh['zh'=8,'zl'=2,'x'=4,'c'=8] {'zh','zl'}, dimensions={0} | all-to-all | bytes 425984 | tf_op jit(solution)/shard_map/all_to_all | solution.py:20
  46.9 0.1 copy.10.got
  47.0 0.4 shard_map.88
  47.3 13.0 %all_to_all.37.parts = f32[8,64,128]{2,1,0:T(8,128)S(1)} all-to-all(f32[8,64,128]{2,1,0:T(8,128)S(1)} %shard_map.88), channel_id=1, replica_groups=mesh['zh'=8,'zl'=2,'x'=4,'c'=8] {'c'}, dimensions={0} | all-to-all | bytes 524288 | tf_op jit(solution)/shard_map/all_to_all | solution.py:20
  60.4 0.3 shard_map.89
  60.7 0.0 copy-start
  60.7 10.1 %all_to_all.38.parts = f32[8,64,128]{2,1,0:T(8,128)S(1)} all-to-all(f32[8,64,128]{2,1,0:T(8,128)S(1)} %get-tuple-element.6), channel_id=1, replica_groups=mesh['zh'=8,'zl'=2,'x'=4,'c'=8] {'x','zl'}, dimensions={0} | all-to-all | bytes 524288 | tf_op jit(solution)/shard_map/all_to_all | solution.py:20
  70.8 0.4 shard_map.90
  71.2 10.1 %all_to_all.39.parts = f32[8,32,128]{2,1,0:T(8,128)S(1)} all-to-all(f32[8,32,128]{2,1,0:T(8,128)S(1)} %shard_map.90), channel_id=1, replica_groups=mesh['zh'=8,'zl'=2,'x'=4,'c'=8] {'c'}, dimensions={0} | all-to-all | bytes 262144 | tf_op jit(solution)/shard_map/all_to_all | solution.py:20
  81.3 7.8 %all_to_all.40.parts = f32[8,24,128]{2,1,0:T(8,128)S(1)} all-to-all(f32[8,24,128]{2,1,0:T(8,128)S(1)} %shard_map.91), channel_id=1, replica_groups=mesh['zh'=8,'zl'=2,'x'=4,'c'=8] {'x','zl'}, dimensions={0} | all-to-all | bytes 196608 | tf_op jit(solution)/shard_map/all_to_all | solution.py:20
  89.1 0.0 copy-done
  89.1 0.5 shard_map.92
  89.6 0.0 copy-start.1
  89.6 14.1 %all_to_all.41.got = f32[8,64,256]{2,1,0:T(8,128)S(1)} all-to-all(f32[8,64,256]{2,1,0:T(8,128)S(1)} %shard_map.92), channel_id=1, replica_groups=mesh['zh'=8,'zl'=2,'x'=4,'c'=8] {'c'}, dimensions={0} | all-to-all | bytes 1048576 | tf_op jit(solution)/shard_map/all_to_all | solution.py:20
  103.7 0.0 copy-done.1
  103.7 0.7 shard_map.93
  (2 shorter events, 0.0 us)
Async XLA Ops:
  60.7 28.4 %copy-start = (bf16[2048,256]{1,0:T(8,128)(2,1)S(1)}, bf16[2048,256]{1,0:T(8,128)(2,1)}, u32[]{:S(2)}) copy-start(bf16[2048,256]{1,0:T(8,128)(2,1)} %design.1) | copy-start | bytes 3145732
  89.6 14.1 %copy-start.1 = (f32[256,64]{0,1:T(8,128)S(1)}, f32[256,64]{0,1:T(8,128)}, u32[]{:S(2)}) copy-start(f32[256,64]{0,1:T(8,128)} %param.13) | copy-start | bytes 196612

commit v13 on v11

--- a/solution.py
+++ b/solution.py
@@ -157,12 +157,11 @@
         near = jnp.where(lax.axis_index("zh") < 4, near, right)
         piece = own[:, 64 * h : 64 * h + 64]
         piece = jnp.concatenate([piece[0:1], piece[1:2]], axis=1)
-        piece = jnp.concatenate([piece, piece], axis=0)
         for k in range(8):
             for m, tile in enumerate((near, far, halves[h])):
-                for j in range(4):
-                    out[2 * k + h, 4 * m + j] = tile[2 * j : 2 * j + 2]
-            out[2 * k + h, 12] = piece
+                for j in range(8):
+                    out[2 * k + h, 8 * m + j] = tile[j : j + 1]
+            out[2 * k + h, 24] = piece
 
 
 def applied(got, lanes, vector):
@@ -270,7 +269,7 @@
     )
     got = exchange(message, ("x", "c"))
 
-    got = exchange(call(split_body, f32(16, 13, 2, 128), got), ("zh", "zl")).reshape(16, 26, 128)
+    got = exchange(call(split_body, f32(16, 25, 1, 128), got), ("zh", "zl")).reshape(16, 25, 128)
 
     parts = exchange(call(last_body, f32(8, 64, 128), got), "c")
 

time: 105 us -> 104 us (level)
  no operation moved by 1% of the time
where the time goes in v13:
time: 104 us
  blocking collectives  98.5 us (95%)
  Pallas kernels  4.66 us (4%)
    all_to_all x7, blocking collectives, exchange(): return lax.all_to_all(value, axes, 0, 0, tiled=True)  98.5 us
    pallas_call x8, Pallas kernels, call(): pl.pallas_call(body, out_shape=out, in_specs=specs or [VMEM] * len(args),...  4.66 us

profile of v13, /device:TPU:1, one launch (start us, length us, event | category | flops | bytes accessed | tf_op | source)
XLA Modules:
  0.0 103.9 jit_solution(9211877426522800235)
XLA Ops:
  0.6 2.1 %shard_map.86 = f32[32,8,128]{2,1,0:T(8,128)S(1)} custom-call(f32[32,4096]{1,0:T(8,128)} %panel_hbm.1, f32[64,4096]{1,0:T(8,128)} %bitcast.11, f32[32,64]{1,0:T(8,128)} %sketch_hbm.1, f32[2,16,128]{2,1,0:T(8,128)} %inverses_hbm.1, f32[16,128]{1,0:T(8,128)} %coupling_hbm.1), custom_call_target="tpu_custom_call" | custom-call | tf_op jit(solution)/shard_map/pallas_call | solution.py:33
  2.7 17.3 %all_to_all.35.got = f32[32,8,128]{2,1,0:T(8,128)S(1)} all-to-all(f32[32,8,128]{2,1,0:T(8,128)S(1)} %shard_map.86), channel_id=1, replica_groups=mesh['zh'=8,'zl'=2,'x'=4,'c'=8] {'x','c'}, dimensions={0} | all-to-all | bytes 262144 | tf_op jit(solution)/shard_map/all_to_all | solution.py:20
  20.0 0.3 shard_map.87
  20.3 26.5 %all_to_all.36 = f32[16,25,1,128]{3,2,1,0:T(1,128)S(1)} all-to-all(f32[16,25,1,128]{3,2,1,0:T(1,128)S(1)} %shard_map.87), channel_id=1, replica_groups=mesh['zh'=8,'zl'=2,'x'=4,'c'=8] {'zh','zl'}, dimensions={0} | all-to-all | bytes 409600 | tf_op jit(solution)/shard_map/all_to_all | solution.py:20
  46.8 0.4 shard_map.88
  47.2 12.8 %all_to_all.37.parts = f32[8,64,128]{2,1,0:T(8,128)S(1)} all-to-all(f32[8,64,128]{2,1,0:T(8,128)S(1)} %shard_map.88), channel_id=1, replica_groups=mesh['zh'=8,'zl'=2,'x'=4,'c'=8] {'c'}, dimensions={0} | all-to-all | bytes 524288 | tf_op jit(solution)/shard_map/all_to_all | solution.py:20
  60.0 0.3 shard_map.89
  60.3 0.0 copy-start
  60.3 10.1 %all_to_all.38.parts = f32[8,64,128]{2,1,0:T(8,128)S(1)} all-to-all(f32[8,64,128]{2,1,0:T(8,128)S(1)} %get-tuple-element.6), channel_id=1, replica_groups=mesh['zh'=8,'zl'=2,'x'=4,'c'=8] {'zl','x'}, dimensions={0} | all-to-all | bytes 524288 | tf_op jit(solution)/shard_map/all_to_all | solution.py:20
  70.4 0.4 shard_map.90
  70.8 10.1 %all_to_all.39.parts = f32[8,32,128]{2,1,0:T(8,128)S(1)} all-to-all(f32[8,32,128]{2,1,0:T(8,128)S(1)} %shard_map.90), channel_id=1, replica_groups=mesh['zh'=8,'zl'=2,'x'=4,'c'=8] {'c'}, dimensions={0} | all-to-all | bytes 262144 | tf_op jit(solution)/shard_map/all_to_all | solution.py:20
  80.9 7.7 %all_to_all.40.parts = f32[8,24,128]{2,1,0:T(8,128)S(1)} all-to-all(f32[8,24,128]{2,1,0:T(8,128)S(1)} %shard_map.91), channel_id=1, replica_groups=mesh['zh'=8,'zl'=2,'x'=4,'c'=8] {'zl','x'}, dimensions={0} | all-to-all | bytes 196608 | tf_op jit(solution)/shard_map/all_to_all | solution.py:20
  88.6 0.0 copy-done
  88.6 0.5 shard_map.92
  89.1 0.0 copy-start.1
  89.1 14.1 %all_to_all.41.got = f32[8,64,256]{2,1,0:T(8,128)S(1)} all-to-all(f32[8,64,256]{2,1,0:T(8,128)S(1)} %shard_map.92), channel_id=1, replica_groups=mesh['zh'=8,'zl'=2,'x'=4,'c'=8] {'c'}, dimensions={0} | all-to-all | bytes 1048576 | tf_op jit(solution)/shard_map/all_to_all | solution.py:20
  103.2 0.0 copy-done.1
  103.2 0.7 shard_map.93
  (2 shorter events, 0.0 us)
Async XLA Ops:
  60.3 28.3 %copy-start = (bf16[2048,256]{1,0:T(8,128)(2,1)S(1)}, bf16[2048,256]{1,0:T(8,128)(2,1)}, u32[]{:S(2)}) copy-start(bf16[2048,256]{1,0:T(8,128)(2,1)} %design.1) | copy-start | bytes 3145732
  89.1 14.1 %copy-start.1 = (f32[256,64]{0,1:T(8,128)S(1)}, f32[256,64]{0,1:T(8,128)}, u32[]{:S(2)}) copy-start(f32[256,64]{0,1:T(8,128)} %param.13) | copy-start | bytes 196612

commit v14 on v13

--- a/solution.py
+++ b/solution.py
@@ -88,7 +88,8 @@
         kept = jnp.where(group == (c2 + row) % 8, both, 0.0)
         kept = kept.reshape(4, 8, 128).sum(axis=1)
         for x2 in range(4):
-            out[8 * x2 + c2, 2:6] = kept
+            for j in range(4):
+                out[8 * x2 + c2, 2 + j] = kept[j : j + 1]
 
     copies[1].wait()
     couple = permuted(
@@ -101,10 +102,8 @@
         kept = jnp.where(group == (x2 + row) % 4, couple, 0.0)
         for g in range(4):
             piece = jnp.sum(jnp.where(row // 4 == g, kept, 0.0), axis=0, keepdims=True)
-            out[8 * x2 + g, 6:7] = piece
-            out[8 * x2 + 4 + g, 6:7] = piece
-            out[8 * x2 + g, 7:8] = piece
-            out[8 * x2 + 4 + g, 7:8] = piece
+            out[8 * x2 + g, 6] = piece
+            out[8 * x2 + 4 + g, 6] = piece
 
     copies[2].wait()
     products = jnp.zeros((64, 128), jnp.float32)
@@ -120,7 +119,8 @@
     for c2 in range(8):
         piece = packed(total[4 * c2 : 4 * c2 + 4])
         for x2 in range(4):
-            out[8 * x2 + c2, 0:2] = piece
+            out[8 * x2 + c2, 0] = piece[0:1]
+            out[8 * x2 + c2, 1] = piece[1:2]
 
 
 def split_body(got, out):
@@ -143,7 +143,7 @@
     halves = [jnp.zeros((8, 128), jnp.float32) for _ in range(2)]
     for a in range(2):
         for c1 in range(8):
-            piece = got[8 * (c // 4 + 2 * a) + c1, 6:8]
+            piece = got[8 * (c // 4 + 2 * a) + c1, 6:7]
             piece = pltpu.roll(piece, (16 * c1 + 128 - 32 * x) % 128, 1)[:1]
             for h in range(2):
                 here = (group == (2 * row + h + c1) % 8) & (row // 4 == a)
@@ -252,7 +252,7 @@
 def local(panel, solved, sketch, inverses, coupling, design, prior):
     message = call(
         start_body,
-        f32(32, 8, 128),
+        f32(32, 7, 1, 128),
         *(
             pltpu.with_memory_space_constraint(value, pltpu.HBM)
             for value in (panel, solved.T, sketch, inverses, coupling)
@@ -267,7 +267,7 @@
             pltpu.SemaphoreType.DMA((3 + 2 * CHUNKS,)),
         ],
     )
-    got = exchange(message, ("x", "c"))
+    got = exchange(message, ("x", "c")).reshape(32, 7, 128)
 
     got = exchange(call(split_body, f32(16, 25, 1, 128), got), ("zh", "zl")).reshape(16, 25, 128)
 

time: 104 us -> 104 us (level)
  no operation moved by 1% of the time
where the time goes in v14:
time: 104 us
  blocking collectives  98.4 us (95%)
  Pallas kernels  4.67 us (4%)
    all_to_all x7, blocking collectives, exchange(): return lax.all_to_all(value, axes, 0, 0, tiled=True)  98.4 us
    pallas_call x8, Pallas kernels, call(): pl.pallas_call(body, out_shape=out, in_specs=specs or [VMEM] * len(args),...  4.67 us

profile of v14, /device:TPU:1, one launch (start us, length us, event | category | flops | bytes accessed | tf_op | source)
XLA Modules:
  0.0 103.8 jit_solution(202234665155569789)
XLA Ops:
  0.6 2.1 %shard_map.86 = f32[32,7,1,128]{3,2,1,0:T(1,128)S(1)} custom-call(f32[32,4096]{1,0:T(8,128)} %panel_hbm.1, f32[64,4096]{1,0:T(8,128)} %bitcast.16, f32[32,64]{1,0:T(8,128)} %sketch_hbm.1, f32[2,16,128]{2,1,0:T(8,128)} %inverses_hbm.1, f32[16,128]{1,0:T(8,128)} %coupling_hbm.1), custom_call_target="tpu_custom_call" | custom-call | tf_op jit(solution)/shard_map/pallas_call | solution.py:33
  2.7 17.2 %all_to_all.35 = f32[32,7,1,128]{3,2,1,0:T(1,128)S(1)} all-to-all(f32[32,7,1,128]{3,2,1,0:T(1,128)S(1)} %shard_map.86), channel_id=1, replica_groups=mesh['zh'=8,'zl'=2,'x'=4,'c'=8] {'x','c'}, dimensions={0} | all-to-all | bytes 229376 | tf_op jit(solution)/shard_map/all_to_all | solution.py:20
  19.9 0.3 shard_map.87
  20.2 26.5 %all_to_all.36 = f32[16,25,1,128]{3,2,1,0:T(1,128)S(1)} all-to-all(f32[16,25,1,128]{3,2,1,0:T(1,128)S(1)} %shard_map.87), channel_id=1, replica_groups=mesh['zh'=8,'zl'=2,'x'=4,'c'=8] {'zh','zl'}, dimensions={0} | all-to-all | bytes 409600 | tf_op jit(solution)/shard_map/all_to_all | solution.py:20
  46.7 0.4 shard_map.88
  47.1 12.8 %all_to_all.37.parts = f32[8,64,128]{2,1,0:T(8,128)S(1)} all-to-all(f32[8,64,128]{2,1,0:T(8,128)S(1)} %shard_map.88), channel_id=1, replica_groups=mesh['zh'=8,'zl'=2,'x'=4,'c'=8] {'c'}, dimensions={0} | all-to-all | bytes 524288 | tf_op jit(solution)/shard_map/all_to_all | solution.py:20
  59.8 0.3 shard_map.89
  60.2 0.0 copy-start
  60.2 10.1 %all_to_all.38.parts = f32[8,64,128]{2,1,0:T(8,128)S(1)} all-to-all(f32[8,64,128]{2,1,0:T(8,128)S(1)} %get-tuple-element.6), channel_id=1, replica_groups=mesh['zh'=8,'zl'=2,'x'=4,'c'=8] {'zl','x'}, dimensions={0} | all-to-all | bytes 524288 | tf_op jit(solution)/shard_map/all_to_all | solution.py:20
  70.3 0.4 shard_map.90
  70.7 10.1 %all_to_all.39.parts = f32[8,32,128]{2,1,0:T(8,128)S(1)} all-to-all(f32[8,32,128]{2,1,0:T(8,128)S(1)} %shard_map.90), channel_id=1, replica_groups=mesh['zh'=8,'zl'=2,'x'=4,'c'=8] {'c'}, dimensions={0} | all-to-all | bytes 262144 | tf_op jit(solution)/shard_map/all_to_all | solution.py:20
  80.8 7.7 %all_to_all.40.parts = f32[8,24,128]{2,1,0:T(8,128)S(1)} all-to-all(f32[8,24,128]{2,1,0:T(8,128)S(1)} %shard_map.91), channel_id=1, replica_groups=mesh['zh'=8,'zl'=2,'x'=4,'c'=8] {'zl','x'}, dimensions={0} | all-to-all | bytes 196608 | tf_op jit(solution)/shard_map/all_to_all | solution.py:20
  88.5 0.0 copy-done
  88.5 0.5 shard_map.92
  89.0 0.0 copy-start.1
  89.0 14.1 %all_to_all.41.got = f32[8,64,256]{2,1,0:T(8,128)S(1)} all-to-all(f32[8,64,256]{2,1,0:T(8,128)S(1)} %shard_map.92), channel_id=1, replica_groups=mesh['zh'=8,'zl'=2,'x'=4,'c'=8] {'c'}, dimensions={0} | all-to-all | bytes 1048576 | tf_op jit(solution)/shard_map/all_to_all | solution.py:20
  103.1 0.0 copy-done.1
  103.1 0.7 shard_map.93
  (3 shorter events, 0.0 us)
Async XLA Ops:
  60.2 28.3 %copy-start = (bf16[2048,256]{1,0:T(8,128)(2,1)S(1)}, bf16[2048,256]{1,0:T(8,128)(2,1)}, u32[]{:S(2)}) copy-start(bf16[2048,256]{1,0:T(8,128)(2,1)} %design.1) | copy-start | bytes 3145732
  89.0 14.1 %copy-start.1 = (f32[256,64]{0,1:T(8,128)S(1)}, f32[256,64]{0,1:T(8,128)}, u32[]{:S(2)}) copy-start(f32[256,64]{0,1:T(8,128)} %param.13) | copy-start | bytes 196612
